TPU v7x, 256 devices: a whole 4x4x8 slice. The times are simulated.
256 devices in a mesh: section: 16 (over z, x_hi), peer: 16 (over y, x_lo, core).
Axes of the slice: x: 4 (x_hi: 2, x_lo: 2; x = x_hi * 2 + x_lo), y: 4, z: 8, core: 2. Of those that a mesh axis runs over, the one named last changes fastest.
Arguments:
- carried: bfloat16 [16, 16, 64, 5120], P('section', 'peer'), may hold values from -60 to 60
- pending: bfloat16 [16, 16, 64, 5120], P('section', 'peer'), may hold values from -6 to 6
- stashed_inputs: bfloat16 [16, 16, 4, 64, 5120], P('section', 'peer'), may hold values from -60 to 60
- fresh_batches: bfloat16 [3, 16, 64, 5120], P(None, 'peer'), may hold values from -60 to 60
- cotangent: bfloat16 [4, 16, 64, 5120], P(None, 'peer'), may hold values from -6 to 6
- norm_gain: float32 [16, 5120], P('section'), may hold values from 0.1 to 1.9
- w_down: bfloat16 [16, 5120, 256], P('section', 'peer'), may hold values from -0.078125 to 0.078125
- w_up: bfloat16 [16, 256, 5120], P('section', None, 'peer'), may hold values from -0.375 to 0.375
- forward_route: int32 [3, 15, 16], replicated, may hold values from 0 to 15, each once within a row
- backward_route: int32 [3, 15, 16], replicated, may hold values from 0 to 15, each once within a row
Outputs:
- outgoing: bfloat16 [16, 16, 64, 5120], P('section', 'peer')
- returning: bfloat16 [16, 16, 64, 5120], P('section', 'peer')
- grad_down: float32 [16, 5120, 256], P('section', 'peer')
- grad_up: float32 [16, 256, 5120], P('section', None, 'peer')
Inputs may be any that keep to these rules, and one draw needn't show every extreme that they name: `forward_route`: each row along the last dimension names each of the 16 peers once. `backward_route`: each row along the last dimension names each of the 16 peers once.
All inputs are finite; a program needn't handle non-finite values.
Results may differ from a plain program's by a relative error of at most 0.023.
Values may be sent and summed in bfloat16 or wider, within the bound.
A program may use at most 128 MiB of HBM per device.

v0:
```python
import jax
import jax.numpy as jnp
from jax import lax
from jax.sharding import PartitionSpec as P

NORM_EPS = 1e-05


def passed_along(value, axis, by):
    length = lax.axis_size(axis)
    pairs = [(i, i + by) for i in range(length) if 0 <= i + by < length]
    return lax.ppermute(value, axis, pairs)


def norm_parts(rows_in, gain_row):
    input_float = rows_in.astype(jnp.float32)
    norm_scale = lax.rsqrt(jnp.mean(input_float * input_float, axis=-1, keepdims=True) + NORM_EPS)
    normed = (input_float * norm_scale * gain_row).astype(jnp.bfloat16)
    return (input_float, norm_scale, normed)


def section_forward(rows_in, gain_row, down_matrix, up_matrix):
    input_float, norm_scale, normed = norm_parts(rows_in, gain_row)
    latent = jnp.dot(normed, down_matrix, preferred_element_type=jnp.float32)
    hidden = (latent * jax.nn.sigmoid(latent)).astype(jnp.bfloat16)
    result = input_float + jnp.dot(hidden, up_matrix, preferred_element_type=jnp.float32)
    return result.astype(jnp.bfloat16)


def section_backward(rows_in, output_grad, gain_row, down_matrix, up_matrix):
    input_float, norm_scale, normed = norm_parts(rows_in, gain_row)
    latent = jnp.dot(normed, down_matrix, preferred_element_type=jnp.float32)
    sigmoid_latent = jax.nn.sigmoid(latent)
    hidden = (latent * sigmoid_latent).astype(jnp.bfloat16)
    hidden_grad = lax.dot_general(
        output_grad, up_matrix, (((1,), (1,)), ((), ())), preferred_element_type=jnp.float32
    )
    latent_grad = (hidden_grad * sigmoid_latent * (1.0 + latent * (1.0 - sigmoid_latent))).astype(
        jnp.bfloat16
    )
    normed_grad = lax.dot_general(
        latent_grad, down_matrix, (((1,), (1,)), ((), ())), preferred_element_type=jnp.float32
    )
    scaled = normed_grad * gain_row
    cubed = norm_scale * norm_scale * norm_scale
    input_grad = (
        output_grad.astype(jnp.float32)
        + norm_scale * scaled
        - input_float * cubed * jnp.mean(scaled * input_float, axis=-1, keepdims=True)
    )
    return (input_grad.astype(jnp.bfloat16), normed, latent_grad, hidden)


def section_step(payload, onward):
    if onward:
        return passed_along(payload, "section", 1)
    return passed_along(payload, "section", -1)


def route_hop(payload, matchings, section_index, section_count, onward):
    peer_count = lax.axis_size("peer")
    row_count, feature_count = payload.shape
    pieces = lax.all_to_all(
        payload.reshape(peer_count, row_count // peer_count, feature_count),
        "peer",
        split_axis=0,
        concat_axis=0,
        tiled=True,
    )
    if onward:
        boundary = section_index
    else:
        boundary = section_index - 1
    boundary = jnp.clip(boundary, 0, section_count - 2)
    matching = lax.dynamic_index_in_dim(matchings, boundary, 0, keepdims=False)
    inverse = (
        jnp.zeros((peer_count,), jnp.int32)
        .at[matching]
        .set(jnp.arange(peer_count, dtype=jnp.int32))
    )
    pieces = jnp.take(pieces, inverse, axis=0)
    pieces = section_step(pieces, onward)
    arrived = lax.all_to_all(pieces, "peer", split_axis=0, concat_axis=0, tiled=True)
    return arrived.reshape(row_count, feature_count)


def shards(
    carried,
    pending,
    stashed_inputs,
    fresh_batches,
    cotangent,
    norm_gain,
    w_down,
    w_up,
    forward_route,
    backward_route,
):
    section_count = lax.axis_size("section")
    section_index = lax.axis_index("section")
    tick_count = stashed_inputs.shape[2]
    down_full, up_full = (
        lax.all_gather(w_down[0], "peer", axis=0, tiled=True),
        lax.all_gather(w_up[0], "peer", axis=1, tiled=True),
    )
    gain_row = norm_gain[0]
    is_first = section_index == 0
    is_last = section_index == section_count - 1
    activations = carried[0, 0]
    grads_in = pending[0, 0]
    outgoing = activations
    returning = grads_in
    down_total = jnp.zeros(down_full.shape, jnp.float32)
    up_total = jnp.zeros(up_full.shape, jnp.float32)
    for tick_index in range(tick_count):
        if tick_index > 0:
            arrived = route_hop(
                outgoing, forward_route[tick_index - 1], section_index, section_count, True
            )
            activations = jnp.where(is_first, fresh_batches[tick_index - 1, 0], arrived)
            grads_in = route_hop(
                returning, backward_route[tick_index - 1], section_index, section_count, False
            )
        output_grad = jnp.where(is_last, cotangent[tick_index, 0], grads_in)
        backward_input = jnp.where(is_last, activations, stashed_inputs[0, 0, tick_index])
        outgoing = section_forward(activations, gain_row, down_full, up_full)
        returning, normed, latent_grad, hidden = section_backward(
            backward_input, output_grad, gain_row, down_full, up_full
        )
        down_total = down_total + lax.dot_general(
            normed, latent_grad, (((0,), (0,)), ((), ())), preferred_element_type=jnp.float32
        )
        up_total = up_total + lax.dot_general(
            hidden, output_grad, (((0,), (0,)), ((), ())), preferred_element_type=jnp.float32
        )
    down_share, up_share = (
        lax.psum_scatter(
            down_total.astype(jnp.bfloat16), "peer", scatter_dimension=0, tiled=True
        ).astype(jnp.float32),
        lax.psum_scatter(
            up_total.astype(jnp.bfloat16), "peer", scatter_dimension=1, tiled=True
        ).astype(jnp.float32),
    )
    return (outgoing[None, None], returning[None, None], down_share[None], up_share[None])


def solution(mesh):
    in_specs = (
        P("section", "peer", None, None),
        P("section", "peer", None, None),
        P("section", "peer", None, None, None),
        P(None, "peer", None, None),
        P(None, "peer", None, None),
        P("section", None),
        P("section", "peer", None),
        P("section", None, "peer"),
        P(),
        P(),
    )
    out_specs = (
        P("section", "peer", None, None),
        P("section", "peer", None, None),
        P("section", "peer", None),
        P("section", None, "peer"),
    )
    return jax.shard_map(shards, mesh=mesh, in_specs=in_specs, out_specs=out_specs, check_vma=False)
```

profile of v0, /device:TPU:4, one launch (start us, length us, event | category | flops | bytes accessed | tf_op | source)
XLA Modules:
  0.0 570.9 jit_solution(1151713057469442275)
XLA Ops:
  15.0 35.1 %all-gather.7.cloned.1.call-done = bf16[1,256,5120]{1,2,0:T(8,128)(2,1)} async-done(((bf16[1,256,320]{1,2,0:T(8,128)(2,1)}), bf16[1,256,5120]{1,2,0:T(8,128)(2,1)}) %all-gather.7.cloned.1.call-update) | async-done | bytes 2621456 | tf_op jit(solution)/shard_map/all_gather | solution.py:104
  50.1 39.5 %all-gather.5.cloned.1.call-done = bf16[1,5120,256]{2,1,0:T(8,128)(2,1)} async-done(((bf16[1,320,256]{2,1,0:T(8,128)(2,1)}), bf16[1,5120,256]{2,1,0:T(8,128)(2,1)}) %all-gather.5.cloned.1.call-update) | async-done | bytes 2621456 | tf_op jit(solution)/shard_map/all_gather | solution.py:103
  89.6 4.6 fusion.3
  100.4 11.0 %all-to-all-done = bf16[16,4,5120]{2,1,0:T(4,128)(2,1)S(1)} async-done(((bf16[16,4,5120]{2,1,0:T(4,128)(2,1)}), bf16[16,4,5120]{2,1,0:T(4,128)(2,1)S(1)}, u32[]{:S(2)}, u32[]{:S(2)}) %all-to-all-start) | async-done | bytes 655392 | tf_op jit(solution)/shard_map/all_to_all | solution.py:63
  116.6 15.7 %collective-permute-done = bf16[16,4,5120]{2,1,0:T(4,128)(2,1)} collective-permute-done((bf16[16,4,5120]{2,1,0:T(4,128)(2,1)S(1)}, bf16[16,4,5120]{2,1,0:T(4,128)(2,1)}, u32[]{:S(2)}, u32[]{:S(2)}) %collective-permute-start) | collective-permute-done | bytes 655392 | tf_op jit(solution)/shard_map/ppermute | solution.py:12
  137.3 10.9 %all-to-all-done.1 = bf16[16,4,5120]{2,1,0:T(4,128)(2,1)S(1)} async-done(((bf16[16,4,5120]{2,1,0:T(4,128)(2,1)}), bf16[16,4,5120]{2,1,0:T(4,128)(2,1)S(1)}, u32[]{:S(2)}, u32[]{:S(2)}) %all-to-all-start.1) | async-done | bytes 655392 | tf_op jit(solution)/shard_map/all_to_all | solution.py:83
  163.7 5.0 fusion.4
  171.0 5.0 all-to-all-done.6
  176.0 4.3 all-to-all-start.2
  187.5 5.1 all-to-all-done.2
  197.9 4.8 collective-permute-start.1
  202.8 4.4 collective-permute-done.3
  207.2 5.6 all-to-all-start.7
  213.4 7.8 %collective-permute-done.1 = bf16[16,4,5120]{2,1,0:T(4,128)(2,1)} collective-permute-done((bf16[16,4,5120]{2,1,0:T(4,128)(2,1)}, bf16[16,4,5120]{2,1,0:T(4,128)(2,1)}, u32[]{:S(2)}, u32[]{:S(2)}) %collective-permute-start.1) | collective-permute-done | bytes 655392 | tf_op jit(solution)/shard_map/ppermute | solution.py:12
  225.1 4.3 all-to-all-start.3
  252.1 6.2 %all-to-all-done.8 = bf16[16,4,5120]{2,1,0:T(4,128)(2,1)} async-done(((bf16[16,4,5120]{2,1,0:T(4,128)(2,1)}), bf16[16,4,5120]{2,1,0:T(4,128)(2,1)}, u32[]{:S(2)}, u32[]{:S(2)}) %all-to-all-start.8) | async-done | bytes 655392 | tf_op jit(solution)/shard_map/all_to_all | solution.py:63
  263.7 8.2 %collective-permute-start.4 = (bf16[16,4,5120]{2,1,0:T(4,128)(2,1)}, bf16[16,4,5120]{2,1,0:T(4,128)(2,1)}, u32[]{:S(2)}, u32[]{:S(2)}) collective-permute-start(bf16[16,4,5120]{2,1,0:T(4,128)(2,1)} %broadcast_select_fusion.1), channel_id=1, source_target_pairs={{16,0},{32,16},{48,32},{64,48},{80,64},{96,80},{112,96},{128,112},... | collective-permute-start | bytes 1966088 | tf_op jit(solution)/shard_map/ppermute | solution.py:12
  271.9 5.0 fusion.5
  285.2 10.6 %all-to-all-done.4 = bf16[16,4,5120]{2,1,0:T(4,128)(2,1)} async-done(((bf16[16,4,5120]{2,1,0:T(4,128)(2,1)}), bf16[16,4,5120]{2,1,0:T(4,128)(2,1)}, u32[]{:S(2)}, u32[]{:S(2)}) %all-to-all-start.4) | async-done | bytes 655392 | tf_op jit(solution)/shard_map/all_to_all | solution.py:63
  305.3 11.5 %collective-permute-start.2 = (bf16[16,4,5120]{2,1,0:T(4,128)(2,1)}, bf16[16,4,5120]{2,1,0:T(4,128)(2,1)}, u32[]{:S(2)}, u32[]{:S(2)}) collective-permute-start(bf16[16,4,5120]{2,1,0:T(4,128)(2,1)} %broadcast_select_fusion.3), channel_id=1, source_target_pairs={{0,16},{16,32},{32,48},{48,64},{64,80},{80,96},{96,112},{112,128},... | collective-permute-start | bytes 1966088 | tf_op jit(solution)/shard_map/ppermute | solution.py:12
  327.8 6.5 %all-to-all-start.10 = ((bf16[16,4,5120]{2,1,0:T(4,128)(2,1)}), bf16[16,4,5120]{2,1,0:T(4,128)(2,1)}, u32[]{:S(2)}, u32[]{:S(2)}) async-start(bf16[16,4,5120]{2,1,0:T(4,128)(2,1)} %reshape.345), calls=%async_computation.10 | async-start | bytes 1310720 | tf_op jit(solution)/shard_map/all_to_all | solution.py:63
  334.3 4.4 fusion.139
  338.7 7.9 %all-to-all-done.10 = bf16[16,4,5120]{2,1,0:T(4,128)(2,1)} async-done(((bf16[16,4,5120]{2,1,0:T(4,128)(2,1)}), bf16[16,4,5120]{2,1,0:T(4,128)(2,1)}, u32[]{:S(2)}, u32[]{:S(2)}) %all-to-all-start.10) | async-done | bytes 655392 | tf_op jit(solution)/shard_map/all_to_all | solution.py:63
  356.2 7.4 %collective-permute-start.5 = (bf16[16,4,5120]{2,1,0:T(4,128)(2,1)}, bf16[16,4,5120]{2,1,0:T(4,128)(2,1)}, u32[]{:S(2)}, u32[]{:S(2)}) collective-permute-start(bf16[16,4,5120]{2,1,0:T(4,128)(2,1)} %broadcast_select_fusion), channel_id=1, source_target_pairs={{16,0},{32,16},{48,32},{64,48},{80,64},{96,80},{112,96},{128,112},... | collective-permute-start | bytes 1966088 | tf_op jit(solution)/shard_map/ppermute | solution.py:12
  363.6 5.8 %convolution_add_fusion.4 = f32[5120,256]{1,0:T(8,128)} fusion(f32[5120,256]{1,0:T(8,128)} %fusion.139, bf16[64,256]{1,0:T(8,128)(2,1)S(1)} %copy-done.21, bf16[64,5120]{1,0:T(8,128)(2,1)S(1)} %get-tuple-element.17, f32[64]{0:T(128)S(1)} %get-tuple-element.30, f32[5120]{0:T(1024)S(1)} %bitcast.219), kind=kOutput, calls=%fused_computation.17 | convolution fusion | flops 170393600 | bytes 11194624 | tf_op jit(solution)/shard_map/dot_general | solution.py:130
  374.4 5.5 collective-permute-done.5
  380.0 6.2 %all-to-all-start.11 = ((bf16[16,4,5120]{2,1,0:T(4,128)(2,1)}), bf16[16,4,5120]{2,1,0:T(4,128)(2,1)}, u32[]{:S(2)}, u32[]{:S(2)}) async-start(bf16[16,4,5120]{2,1,0:T(4,128)(2,1)} %collective-permute-done.5), calls=%async_computation.11 | async-start | bytes 1310720 | tf_op jit(solution)/shard_map/all_to_all | solution.py:83
  387.5 5.8 %convolution_add_fusion.3 = f32[5120,256]{1,0:T(8,128)} fusion(f32[5120,256]{1,0:T(8,128)} %convolution_add_fusion.4, bf16[64,256]{1,0:T(8,128)(2,1)S(1)} %copy-done.23, bf16[64,5120]{1,0:T(8,128)(2,1)S(1)} %copy-done.5, f32[64]{0:T(128)S(1)} %get-tuple-element.28, f32[5120]{0:T(1024)S(1)} %bitcast.221), kind=kOutput, calls=%fused_computation.16 | convolution fusion | flops 170393600 | bytes 11194624 | tf_op jit(solution)/shard_map/dot_general | solution.py:130
  393.3 5.3 all-to-all-done.11
  416.3 5.0 fusion.7
  423.6 68.5 %reduce-scatter.3.cloned.1.call-done = bf16[320,256]{1,0:T(8,128)(2,1)} async-done(((bf16[5120,256]{1,0:T(8,128)(2,1)}), bf16[320,256]{1,0:T(8,128)(2,1)}) %reduce-scatter.3.cloned.1.call-update) | async-done | bytes 163856 | tf_op jit(solution)/shard_map/reduce_scatter | solution.py:137
  493.8 68.5 %reduce-scatter.5.cloned.1.call-done = bf16[256,320]{0,1:T(8,128)(2,1)} async-done(((bf16[256,5120]{0,1:T(8,128)(2,1)}), bf16[256,320]{0,1:T(8,128)(2,1)}) %reduce-scatter.5.cloned.1.call-update) | async-done | bytes 163856 | tf_op jit(solution)/shard_map/reduce_scatter | solution.py:140
  (180 shorter events, 154.6 us)
Async XLA Ops:
  7.2 5.7 %copy-start.18 = (bf16[1,1,64,5120]{3,2,1,0:T(8,128)(2,1)S(1)}, bf16[1,1,64,5120]{3,2,1,0:T(8,128)(2,1)}, u32[]{:S(2)}) copy-start(bf16[1,1,64,5120]{3,2,1,0:T(8,128)(2,1)} %param.13) | copy-start | bytes 1966084
  7.2 42.9 %all-gather.7.cloned.1.call-start = ((), (), s32[]{:S(2)}) async-start(), calls=%async_computation.17 | async-start | bytes 2785280 | tf_op jit(solution)/shard_map/all_gather | solution.py:104
  7.9 81.7 %all-gather.5.cloned.1.call-start = ((), (), s32[]{:S(2)}) async-start(), calls=%async_computation.16 | async-start | bytes 2785280 | tf_op jit(solution)/shard_map/all_gather | solution.py:103
  10.7 78.9 %copy-start.14 = (bf16[1,1,64,5120]{3,2,1,0:T(8,128)(2,1)S(1)}, bf16[1,1,64,5120]{3,2,1,0:T(8,128)(2,1)}, u32[]{:S(2)}) copy-start(bf16[1,1,64,5120]{3,2,1,0:T(8,128)(2,1)} %param.12) | copy-start | bytes 1966084
  10.7 78.9 %copy-start.17 = (f32[1,5120]{1,0:T(1,128)S(1)}, f32[1,5120]{1,0:T(1,128)}, u32[]{:S(2)}) copy-start(f32[1,5120]{1,0:T(1,128)} %param.17) | copy-start | bytes 61444
  95.3 16.1 %all-to-all-start = ((bf16[16,4,5120]{2,1,0:T(4,128)(2,1)}), bf16[16,4,5120]{2,1,0:T(4,128)(2,1)S(1)}, u32[]{:S(2)}, u32[]{:S(2)}) async-start(bf16[16,4,5120]{2,1,0:T(4,128)(2,1)} %reshape.335), calls=%async_computation | async-start | bytes 1310720 | tf_op jit(solution)/shard_map/all_to_all | solution.py:63
  112.8 19.5 %collective-permute-start = (bf16[16,4,5120]{2,1,0:T(4,128)(2,1)S(1)}, bf16[16,4,5120]{2,1,0:T(4,128)(2,1)}, u32[]{:S(2)}, u32[]{:S(2)}) collective-permute-start(bf16[16,4,5120]{2,1,0:T(4,128)(2,1)S(1)} %broadcast_select_fusion.5), channel_id=1, source_target_pairs={{0,16},{16,32},{32,48},{48,64},{64,80},{80,96},{96,112},{112,128},... | collective-permute-start | bytes 1966088 | tf_op jit(solution)/shard_map/ppermute | solution.py:12
  132.3 15.9 %all-to-all-start.1 = ((bf16[16,4,5120]{2,1,0:T(4,128)(2,1)}), bf16[16,4,5120]{2,1,0:T(4,128)(2,1)S(1)}, u32[]{:S(2)}, u32[]{:S(2)}) async-start(bf16[16,4,5120]{2,1,0:T(4,128)(2,1)} %collective-permute-done), calls=%async_computation.1 | async-start | bytes 1310720 | tf_op jit(solution)/shard_map/all_to_all | solution.py:83
  137.2 65.5 %copy-start.24 = (s32[16]{0:T(128)}, s32[16]{0:T(128)S(1)}, u32[]{:S(2)}) copy-start(s32[16]{0:T(128)S(1)} %scatter_custom_fusion.5) | copy-start | bytes 196
  151.9 4.0 copy-start.3
  159.5 16.6 %all-to-all-start.6 = ((bf16[16,4,5120]{2,1,0:T(4,128)(2,1)}), bf16[16,4,5120]{2,1,0:T(4,128)(2,1)}, u32[]{:S(2)}, u32[]{:S(2)}) async-start(bf16[16,4,5120]{2,1,0:T(4,128)(2,1)} %reshape.341), calls=%async_computation.6 | async-start | bytes 1310720 | tf_op jit(solution)/shard_map/all_to_all | solution.py:63
  176.0 16.6 %all-to-all-start.2 = ((bf16[16,4,5120]{2,1,0:T(4,128)(2,1)}), bf16[16,4,5120]{2,1,0:T(4,128)(2,1)}, u32[]{:S(2)}, u32[]{:S(2)}) async-start(bf16[16,4,5120]{2,1,0:T(4,128)(2,1)} %reshape.337), calls=%async_computation.2 | async-start | bytes 1310720 | tf_op jit(solution)/shard_map/all_to_all | solution.py:63
  185.6 21.6 %collective-permute-start.3 = (bf16[16,4,5120]{2,1,0:T(4,128)(2,1)}, bf16[16,4,5120]{2,1,0:T(4,128)(2,1)}, u32[]{:S(2)}, u32[]{:S(2)}) collective-permute-start(bf16[16,4,5120]{2,1,0:T(4,128)(2,1)} %broadcast_select_fusion.2), channel_id=1, source_target_pairs={{16,0},{32,16},{48,32},{64,48},{80,64},{96,80},{112,96},{128,112},... | collective-permute-start | bytes 1966088 | tf_op jit(solution)/shard_map/ppermute | solution.py:12
  197.9 23.3 %collective-permute-start.1 = (bf16[16,4,5120]{2,1,0:T(4,128)(2,1)}, bf16[16,4,5120]{2,1,0:T(4,128)(2,1)}, u32[]{:S(2)}, u32[]{:S(2)}) collective-permute-start(bf16[16,4,5120]{2,1,0:T(4,128)(2,1)} %broadcast_select_fusion.4), channel_id=1, source_target_pairs={{0,16},{16,32},{32,48},{48,64},{64,80},{80,96},{96,112},{112,128},... | collective-permute-start | bytes 1966088 | tf_op jit(solution)/shard_map/ppermute | solution.py:12
  207.2 17.9 %all-to-all-start.7 = ((bf16[16,4,5120]{2,1,0:T(4,128)(2,1)}), bf16[16,4,5120]{2,1,0:T(4,128)(2,1)}, u32[]{:S(2)}, u32[]{:S(2)}) async-start(bf16[16,4,5120]{2,1,0:T(4,128)(2,1)} %collective-permute-done.3), calls=%async_computation.7 | async-start | bytes 1310720 | tf_op jit(solution)/shard_map/all_to_all | solution.py:83
  225.1 16.6 %all-to-all-start.3 = ((bf16[16,4,5120]{2,1,0:T(4,128)(2,1)}), bf16[16,4,5120]{2,1,0:T(4,128)(2,1)}, u32[]{:S(2)}, u32[]{:S(2)}) async-start(bf16[16,4,5120]{2,1,0:T(4,128)(2,1)} %collective-permute-done.1), calls=%async_computation.3 | async-start | bytes 1310720 | tf_op jit(solution)/shard_map/all_to_all | solution.py:83
  233.0 3.6 copy-start.10
  241.7 16.6 %all-to-all-start.8 = ((bf16[16,4,5120]{2,1,0:T(4,128)(2,1)}), bf16[16,4,5120]{2,1,0:T(4,128)(2,1)}, u32[]{:S(2)}, u32[]{:S(2)}) async-start(bf16[16,4,5120]{2,1,0:T(4,128)(2,1)} %reshape.343), calls=%async_computation.8 | async-start | bytes 1310720 | tf_op jit(solution)/shard_map/all_to_all | solution.py:63
  263.7 35.1 %collective-permute-start.4 = (bf16[16,4,5120]{2,1,0:T(4,128)(2,1)}, bf16[16,4,5120]{2,1,0:T(4,128)(2,1)}, u32[]{:S(2)}, u32[]{:S(2)}) collective-permute-start(bf16[16,4,5120]{2,1,0:T(4,128)(2,1)} %broadcast_select_fusion.1), channel_id=1, source_target_pairs={{16,0},{32,16},{48,32},{64,48},{80,64},{96,80},{112,96},{128,112},... | collective-permute-start | bytes 1966088 | tf_op jit(solution)/shard_map/ppermute | solution.py:12
  279.2 16.6 %all-to-all-start.4 = ((bf16[16,4,5120]{2,1,0:T(4,128)(2,1)}), bf16[16,4,5120]{2,1,0:T(4,128)(2,1)}, u32[]{:S(2)}, u32[]{:S(2)}) async-start(bf16[16,4,5120]{2,1,0:T(4,128)(2,1)} %reshape.339), calls=%async_computation.4 | async-start | bytes 1310720 | tf_op jit(solution)/shard_map/all_to_all | solution.py:63
  298.7 18.1 %all-to-all-start.9 = ((bf16[16,4,5120]{2,1,0:T(4,128)(2,1)}), bf16[16,4,5120]{2,1,0:T(4,128)(2,1)}, u32[]{:S(2)}, u32[]{:S(2)}) async-start(bf16[16,4,5120]{2,1,0:T(4,128)(2,1)} %collective-permute-done.4), calls=%async_computation.9 | async-start | bytes 1310720 | tf_op jit(solution)/shard_map/all_to_all | solution.py:83
  305.3 33.4 %collective-permute-start.2 = (bf16[16,4,5120]{2,1,0:T(4,128)(2,1)}, bf16[16,4,5120]{2,1,0:T(4,128)(2,1)}, u32[]{:S(2)}, u32[]{:S(2)}) collective-permute-start(bf16[16,4,5120]{2,1,0:T(4,128)(2,1)} %broadcast_select_fusion.3), channel_id=1, source_target_pairs={{0,16},{16,32},{32,48},{48,64},{64,80},{80,96},{96,112},{112,128},... | collective-permute-start | bytes 1966088 | tf_op jit(solution)/shard_map/ppermute | solution.py:12
  320.5 3.7 copy-start.12
  325.4 8.9 %copy-start.25 = (s32[16]{0:T(128)S(1)}, s32[16]{0:T(128)}, u32[]{:S(2)}) copy-start(s32[16]{0:T(128)} %copy-done.24) | copy-start | bytes 196
  327.8 18.8 %all-to-all-start.10 = ((bf16[16,4,5120]{2,1,0:T(4,128)(2,1)}), bf16[16,4,5120]{2,1,0:T(4,128)(2,1)}, u32[]{:S(2)}, u32[]{:S(2)}) async-start(bf16[16,4,5120]{2,1,0:T(4,128)(2,1)} %reshape.345), calls=%async_computation.10 | async-start | bytes 1310720 | tf_op jit(solution)/shard_map/all_to_all | solution.py:63
  346.6 22.8 %all-to-all-start.5 = ((bf16[16,4,5120]{2,1,0:T(4,128)(2,1)}), bf16[16,4,5120]{2,1,0:T(4,128)(2,1)}, u32[]{:S(2)}, u32[]{:S(2)}) async-start(bf16[16,4,5120]{2,1,0:T(4,128)(2,1)} %collective-permute-done.2), calls=%async_computation.5 | async-start | bytes 1310720 | tf_op jit(solution)/shard_map/all_to_all | solution.py:83
  350.9 12.7 %copy-start.21 = (bf16[64,256]{1,0:T(8,128)(2,1)S(1)}, bf16[64,256]{1,0:T(8,128)(2,1)}, u32[]{:S(2)}) copy-start(bf16[64,256]{1,0:T(8,128)(2,1)} %copy-done.20) | copy-start | bytes 98308
  356.2 23.8 %collective-permute-start.5 = (bf16[16,4,5120]{2,1,0:T(4,128)(2,1)}, bf16[16,4,5120]{2,1,0:T(4,128)(2,1)}, u32[]{:S(2)}, u32[]{:S(2)}) collective-permute-start(bf16[16,4,5120]{2,1,0:T(4,128)(2,1)} %broadcast_select_fusion), channel_id=1, source_target_pairs={{16,0},{32,16},{48,32},{64,48},{80,64},{96,80},{112,96},{128,112},... | collective-permute-start | bytes 1966088 | tf_op jit(solution)/shard_map/ppermute | solution.py:12
  380.0 18.5 %all-to-all-start.11 = ((bf16[16,4,5120]{2,1,0:T(4,128)(2,1)}), bf16[16,4,5120]{2,1,0:T(4,128)(2,1)}, u32[]{:S(2)}, u32[]{:S(2)}) async-start(bf16[16,4,5120]{2,1,0:T(4,128)(2,1)} %collective-permute-done.5), calls=%async_computation.11 | async-start | bytes 1310720 | tf_op jit(solution)/shard_map/all_to_all | solution.py:83
  386.1 106.0 %reduce-scatter.3.cloned.1.call-start = ((), (), s32[]{:S(2)}) async-start(), calls=%async_computation.14 | async-start | bytes 2785280 | tf_op jit(solution)/shard_map/reduce_scatter | solution.py:137
  400.7 4.7 copy-start.2
  407.9 154.3 %reduce-scatter.5.cloned.1.call-start = ((), (), s32[]{:S(2)}) async-start(), calls=%async_computation.15 | async-start | bytes 2785280 | tf_op jit(solution)/shard_map/reduce_scatter | solution.py:140
  (16 other events, 23.2 us)
Sparse Core Ops, SparseCore 0:
  9.9 40.1 all-gather.6
  51.9 37.6 all-gather.4
  408.1 84.0 reduce-scatter.2
  494.5 67.7 reduce-scatter.4
where the time goes:
time: 582 us; the launch traced here: 571 us
  waiting for transfers between devices  314 us (54%)
  starting transfers between devices  93.4 us (16%)
  matrix products  60.5 us (10%)
  local copies, waits for them, and re-layouts  49.9 us (9%)
  other arithmetic  38.1 us (7%)
  between operations  15.1 us (3%)
    reduce_scatter x1, waiting for transfers between devices, shards(): lax.psum_scatter(down_total.astype(jnp.bfloat16), 'peer', scatter_dimensi...  68.5 us
    reduce_scatter x1, waiting for transfers between devices, shards(): lax.psum_scatter(up_total.astype(jnp.bfloat16), 'peer', scatter_dimension...  68.5 us
    all_to_all x6, waiting for transfers between devices, route_hop(): lax.all_to_all(payload.reshape(peer_count, row_count // peer_count, featu...  45.9 us
    all_gather x1, waiting for transfers between devices, shards(): lax.all_gather(w_down[0], 'peer', axis=0, tiled=True)  39.5 us
    ppermute x6, starting transfers between devices, passed_along(): return lax.ppermute(value, axis, pairs)  37.6 us
    all_gather x1, waiting for transfers between devices, shards(): lax.all_gather(w_up[0], 'peer', axis=1, tiled=True)  35.1 us
    ppermute x6, waiting for transfers between devices, passed_along(): return lax.ppermute(value, axis, pairs)  33.5 us
    all_to_all x6, starting transfers between devices, route_hop(): lax.all_to_all(pieces, 'peer', split_axis=0, concat_axis=0, tiled=True)  28.1 us
  transfers between devices with their start and end apart: 22, of which 18 were waited for; matrix products, arithmetic and copies ran while one was open for 20% of the time, Pallas kernels for 0%

commit v1 on v0

v1 whole, which is shorter than its diff:
```python
import functools

import jax
import jax.numpy as jnp
from jax import lax
from jax.experimental import pallas as pl
from jax.experimental.pallas import tpu as pltpu
from jax.sharding import PartitionSpec as P

MESH = pl.DeviceIdType.MESH
NORM_EPS = 1e-05
TICKS = 4
XS = 4
YS = 4
PEERS = 16
LANES = 128


def high_low(value):
    high = value.astype(jnp.bfloat16).astype(jnp.float32)
    return high, value - high


def kernel(
    planes,
    width,
    inverse,
    carried,
    pending,
    stash,
    fresh,
    cotangent,
    w_down,
    w_up,
    out_ref,
    ret_ref,
    grad_ref,
    x_now,
    v_now,
    u_all,
    fresh_all,
    x_in,
    v_in,
    x_out,
    v_out,
    part_send,
    part_recv,
    rows_all,
    down_all,
    up_all,
    grad_sum,
    grad_send,
    grad_recv,
    spread_send,
    spread_recv,
    part_sems,
    rows_sems,
    hop_send,
    hop_recv,
    last_send,
    last_recv,
):
    section = lax.axis_index("section")
    peer = lax.axis_index("peer")
    z, x_hi = section // 2, section % 2
    y, x_lo, core = peer // 4, (peer // 2) % 2, peer % 2
    x = 2 * x_hi + x_lo
    mine = 2 * z + core
    tokens, columns = x_now.shape[1], x_now.shape[2]
    shard = w_down.shape[0]
    rank = w_down.shape[1]
    rows = PEERS * tokens
    share = rows // YS
    home = core == x_hi
    away = core != x_hi
    is_first = mine == 0
    is_last = mine == 2 * planes - 1
    sends_last = section == 2 * planes - 1

    def place(zz, xx, yy, cc):
        return (2 * zz + xx // 2, 4 * yy + 2 * (xx % 2) + cc)

    def remote(src, dst, send_sem, recv_sem, device):
        pltpu.make_async_remote_copy(
            src_ref=src,
            dst_ref=dst,
            send_sem=send_sem,
            recv_sem=recv_sem,
            device_id=device,
            device_id_type=MESH,
        ).start()

    def settle(ref, sem):
        pltpu.make_async_copy(ref, ref, sem).wait()

    barrier = pltpu.get_barrier_semaphore()
    z_up, z_down = (z + 1) % planes, (z + planes - 1) % planes

    @pl.loop(1, 32)
    def _(i):
        other = (x * 8 + y * 2 + core + i) % 32
        pl.semaphore_signal(
            barrier, inc=1, device_id=place(z, other // 8, (other // 2) % 4, other % 2), device_id_type=MESH
        )

    for zz in (z_up, z_down):
        pl.semaphore_signal(barrier, inc=1, device_id=place(zz, x, y, 1 - core), device_id_type=MESH)
    pl.semaphore_wait(barrier, 33)

    def spread(source, target, send_sem, recv_sem):
        def piece(xx, yy):
            return source.at[
                pl.ds(pl.multiple_of(xx * tokens, tokens), tokens),
                pl.ds(pl.multiple_of(yy * columns, LANES), columns),
            ]

        @pl.when(home)
        def _():
            pltpu.make_async_copy(piece(x, y), target.at[peer], recv_sem).start()

        @pl.when(away)
        def _():
            remote(piece(x, y), target.at[peer], send_sem, recv_sem, place(z, x, y, x_hi))

        @pl.loop(1, XS * YS)
        def _(i):
            xx, yy = (x + i // YS) % XS, (y + i) % YS
            remote(piece(xx, yy), target.at[peer], send_sem, recv_sem, place(z, xx, yy, x_hi))

    def spread_weight(source, target, send_sem, recv_sem):
        block = target.at[pl.ds(pl.multiple_of((2 * x_lo + core) * shard, 16), shard)]

        @pl.when(home)
        def _():
            pltpu.make_async_copy(source, block, recv_sem).start()

        @pl.when(away)
        def _():
            remote(source, block, send_sem, recv_sem, place(z, x, y, x_hi))

        @pl.loop(1, XS)
        def _(i):
            remote(source, block, send_sem, recv_sem, place(z, (x + i) % XS, y, x_hi))

    def settle_sent(ref, count, sem):
        @pl.when(home)
        def _():
            settle(ref.at[pl.ds(0, count - 1)], sem)

        @pl.when(away)
        def _():
            settle(ref.at[pl.ds(0, count)], sem)

    DOWN, CARRIED, UP, PENDING, FRESH, STASH = 0, 1, 2, 3, 4, 5

    def spread_stash(t):
        sems = (spread_send.at[STASH + t], spread_recv.at[STASH + t])

        @pl.when(sends_last)
        def _():
            spread(cotangent.at[t], u_all.at[t], *sems)

        @pl.when(jnp.logical_not(sends_last))
        def _():
            spread(stash.at[t], u_all.at[t], *sems)

    spread_weight(w_down, down_all, spread_send.at[DOWN], spread_recv.at[DOWN])
    spread(carried, x_now, spread_send.at[CARRIED], spread_recv.at[CARRIED])
    spread_weight(w_up, up_all, spread_send.at[UP], spread_recv.at[UP])
    spread(pending, v_now, spread_send.at[PENDING], spread_recv.at[PENDING])
    spread_stash(0)

    def fresh_piece(xx, yy):
        return fresh.at[
            :,
            pl.ds(pl.multiple_of(xx * tokens, tokens), tokens),
            pl.ds(pl.multiple_of(yy * columns, LANES), columns),
        ]

    @pl.when(z == 0)
    def _():
        sems = (spread_send.at[FRESH], spread_recv.at[FRESH])

        @pl.when(core == 0)
        def _():
            pltpu.make_async_copy(fresh_piece(x, y), fresh_all.at[:, peer], sems[1]).start()

        @pl.when(core == 1)
        def _():
            remote(fresh_piece(x, y), fresh_all.at[:, peer], *sems, place(z, x, y, 0))

        @pl.loop(1, 2 * YS)
        def _(i):
            xx, yy = 2 * x_hi + (x_lo + i // YS) % 2, (y + i) % YS
            remote(fresh_piece(xx, yy), fresh_all.at[:, peer], *sems, place(z, xx, yy, 0))

    lane = lax.broadcasted_iota(jnp.int32, (rows, LANES), 1)

    def in_lanes(lane, values):
        result = jnp.zeros(lane.shape, jnp.float32)
        for i, value in enumerate(values):
            result = jnp.where(lane == i, value, result)
        return result.astype(jnp.bfloat16)

    def flat(value):
        return value.reshape(rows, value.shape[-1])

    def square_sum(value):
        value = value.astype(jnp.float32)
        return jnp.sum(value * value, axis=-1, keepdims=True)

    def product(a, b, contract):
        return lax.dot_general(a, b, ((contract[:1], contract[1:]), ((), ())), preferred_element_type=jnp.float32)

    grad_sum[...] = jnp.zeros_like(grad_sum)

    for t in range(TICKS):
        if t > 0:
            settle(x_in[t - 1], hop_recv.at[0, t - 1])
            settle(v_in[t - 1], hop_recv.at[1, t - 1])

            @pl.when(is_first)
            def _():
                if t == 1:
                    settle(fresh_all, spread_recv.at[FRESH])
                x_now[...] = fresh_all[t - 1]

            @pl.when(jnp.logical_not(is_first))
            def _():
                for p in range(PEERS):
                    x_now[p] = x_in[t - 1][inverse[t - 1, p]]

            for p in range(PEERS):
                v_now[p] = v_in[t - 1][inverse[TICKS - 2 + t, p]]
        else:
            settle(down_all, spread_recv.at[DOWN])
            settle(x_now, spread_recv.at[CARRIED])
        x_rows = flat(x_now[...])
        part_send[t, :, :, 0:rank] = (
            product(x_rows, down_all[...], (1, 0)).astype(jnp.bfloat16).reshape(YS, share, rank)
        )
        if t == 0:
            settle(up_all, spread_recv.at[UP])
            settle(v_now, spread_recv.at[PENDING])
        settle(u_all.at[t], spread_recv.at[STASH + t])

        @pl.when(is_last)
        def _():
            v_now[...] = u_all[t]
            u_all[t] = x_now[...]

        part_send[t, :, :, rank : 2 * rank] = (
            product(flat(v_now[...]), up_all[...], (1, 0)).astype(jnp.bfloat16).reshape(YS, share, rank)
        )
        u_rows = flat(u_all[t])
        part_send[t, :, :, 2 * rank : 3 * rank] = (
            product(u_rows, down_all[...], (1, 0)).astype(jnp.bfloat16).reshape(YS, share, rank)
        )
        part_send[t, :, :, 3 * rank :] = in_lanes(
            lane, high_low(square_sum(x_rows)) + high_low(square_sum(u_rows))
        ).reshape(YS, share, LANES)

        for i in range(1, YS):
            yy = (y + i) % YS
            remote(
                part_send.at[t, yy],
                part_recv.at[t, i - 1],
                part_sems.at[0, t],
                part_sems.at[1, t],
                place(z, x, yy, core),
            )
        settle(part_recv.at[t], part_sems.at[1, t])
        total = part_send[t, y].astype(jnp.float32)
        for i in range(YS - 1):
            total = total + part_recv[t, i].astype(jnp.float32)
        extra = total[:, 3 * rank :]
        x_scale = lax.rsqrt((extra[:, 0:1] + extra[:, 1:2]) * (1.0 / width) + NORM_EPS)
        u_scale = lax.rsqrt((extra[:, 2:3] + extra[:, 3:4]) * (1.0 / width) + NORM_EPS)
        latent = total[:, 0:rank] * x_scale
        rows_all[t, y, :, 0:rank] = (latent * jax.nn.sigmoid(latent)).astype(jnp.bfloat16)
        latent = total[:, 2 * rank : 3 * rank] * u_scale
        sigmoid = jax.nn.sigmoid(latent)
        rows_all[t, y, :, 2 * rank : 3 * rank] = (latent * sigmoid).astype(jnp.bfloat16)
        latent_grad = total[:, rank : 2 * rank] * sigmoid * (1.0 + latent * (1.0 - sigmoid))
        rows_all[t, y, :, rank : 2 * rank] = (latent_grad * u_scale).astype(jnp.bfloat16)
        along = jnp.sum(latent_grad * latent, axis=-1, keepdims=True) * (u_scale * u_scale * (1.0 / width))
        rows_all[t, y, :, 3 * rank :] = in_lanes(lane[:share], high_low(along))
        for i in range(1, YS):
            remote(
                rows_all.at[t, y],
                rows_all.at[t, y],
                rows_sems.at[0, t],
                rows_sems.at[1, t],
                place(z, x, (y + i) % YS, core),
            )
        settle(rows_all.at[t, pl.ds(0, YS - 1)], rows_sems.at[1, t])

        hidden = flat(rows_all[t, :, :, 0:rank])
        latent_grad = flat(rows_all[t, :, :, rank : 2 * rank])
        extra = flat(rows_all[t, :, :, 3 * rank :]).astype(jnp.float32)
        along = extra[:, 0:1] + extra[:, 1:2]
        step = 2 * LANES
        for start in range(0, columns, step):
            cut = slice(start, start + step)
            result = flat(x_now[:, :, cut]).astype(jnp.float32) + product(hidden, up_all[cut, :], (1, 1))
            x_out[t, :, :, cut] = result.astype(jnp.bfloat16).reshape(PEERS, tokens, step)
        if t < TICKS - 1:
            remote(
                x_out.at[t],
                x_in[t],
                hop_send.at[0, t],
                hop_recv.at[0, t],
                place((z + core) % planes, x, y, 1 - core),
            )
        for start in range(0, columns, step):
            cut = slice(start, start + step)
            result = (
                flat(v_now[:, :, cut]).astype(jnp.float32)
                + product(latent_grad, down_all[cut, :], (1, 1))
                - flat(u_all[t, :, :, cut]).astype(jnp.float32) * along
            )
            v_out[t, :, :, cut] = result.astype(jnp.bfloat16).reshape(PEERS, tokens, step)
        if t < TICKS - 1:
            remote(
                v_out.at[t],
                v_in[t],
                hop_send.at[1, t],
                hop_recv.at[1, t],
                place((z + core + planes - 1) % planes, x, y, 1 - core),
            )
            spread_stash(t + 1)
        else:
            for k, (source, target) in enumerate(((x_out.at[t], out_ref), (v_out.at[t], ret_ref))):
                block = target.at[
                    pl.ds(pl.multiple_of(x * tokens, tokens), tokens),
                    pl.ds(pl.multiple_of(y * columns, LANES), columns),
                ]

                @pl.when(home)
                def _():
                    pltpu.make_async_copy(source.at[peer], block, last_recv.at[k]).start()

                @pl.when(away)
                def _():
                    remote(source.at[peer], block, last_send.at[k], last_recv.at[k], (mine, peer))

                @pl.loop(1, PEERS)
                def _(i):
                    q = (peer + i) % PEERS
                    remote(source.at[q], block, last_send.at[k], last_recv.at[k], (mine, q))

        hidden = flat(rows_all[t, :, :, 2 * rank : 3 * rank])
        for start in range(0, columns, step):
            cut = slice(start, start + step)
            grad_sum[0, cut, :] += product(flat(u_all[t, :, :, cut]), latent_grad, (0, 0))
            grad_sum[1, cut, :] += product(flat(v_now[:, :, cut]), hidden, (0, 0))

    for q in range(4):
        for k in range(2):
            grad_send[q, k] = grad_sum[k, q * shard : (q + 1) * shard, :].astype(jnp.bfloat16)
    own = 2 * x_lo + core

    @pl.when(home)
    def _():
        pltpu.make_async_copy(grad_send.at[own], grad_recv.at[x], last_recv.at[2]).start()

    @pl.when(away)
    def _():
        remote(grad_send.at[own], grad_recv.at[x], last_send.at[2], last_recv.at[2], (mine, peer))

    @pl.loop(1, 4)
    def _(i):
        q = (own + i) % 4
        remote(grad_send.at[q], grad_recv.at[x], last_send.at[2], last_recv.at[2], (mine, 4 * y + q))

    settle(grad_recv, last_recv.at[2])
    total = grad_recv[0].astype(jnp.float32)
    for i in range(1, XS):
        total = total + grad_recv[i].astype(jnp.float32)
    grad_ref[...] = total

    settle(out_ref, last_recv.at[0])
    settle(ret_ref, last_recv.at[1])

    for k in (DOWN, UP):
        settle_sent(grad_send.at[:, 0], 4, spread_send.at[k])
    for k in (CARRIED, PENDING, *range(STASH, STASH + TICKS)):
        settle_sent(x_now, PEERS, spread_send.at[k])
    for k in range(2):
        settle_sent(x_now, PEERS, last_send.at[k])
    settle_sent(grad_send, 4, last_send.at[2])

    @pl.when(z == 0)
    def _():
        @pl.when(core == 0)
        def _():
            settle(fresh_all.at[:, pl.ds(0, 2 * YS - 1)], spread_send.at[FRESH])

        @pl.when(core == 1)
        def _():
            settle(fresh_all.at[:, pl.ds(0, 2 * YS)], spread_send.at[FRESH])

    for t in range(TICKS):
        settle(part_recv.at[t], part_sems.at[0, t])
        settle(rows_all.at[t, pl.ds(0, YS - 1)], rows_sems.at[0, t])
        if t < TICKS - 1:
            settle(x_out.at[t], hop_send.at[0, t])
            settle(v_out.at[t], hop_send.at[1, t])


def shards(
    planes,
    carried,
    pending,
    stashed_inputs,
    fresh_batches,
    cotangent,
    norm_gain,
    w_down,
    w_up,
    forward_route,
    backward_route,
):
    section = lax.axis_index("section")
    peer = lax.axis_index("peer")
    row_count, width = carried.shape[2:]
    shard, rank = w_down.shape[1:]
    tokens, columns = row_count // XS, width // YS
    rows = PEERS * tokens
    share = rows // YS
    message = 3 * rank + LANES

    mine = 2 * (section // 2) + peer % 2
    boundaries = forward_route.shape[1]
    routes = jnp.concatenate(
        [
            lax.dynamic_index_in_dim(forward_route, jnp.clip(mine - 1, 0, boundaries - 1), 1, keepdims=False),
            lax.dynamic_index_in_dim(backward_route, jnp.clip(mine, 0, boundaries - 1), 1, keepdims=False),
        ]
    )
    places = jnp.arange(PEERS, dtype=jnp.int32)
    inverse = jnp.sum(jnp.where(routes[:, None, :] == places[None, :, None], places[None, None, :], 0), axis=2)

    gain = lax.dynamic_slice_in_dim(norm_gain[0], peer * shard, shard, 0)[:, None]
    down_gained = (w_down[0].astype(jnp.float32) * gain).astype(jnp.bfloat16)
    up_turned = w_up[0].T

    block = (PEERS, tokens, columns)
    bf16, f32 = jnp.bfloat16, jnp.float32
    dma = pltpu.SemaphoreType.DMA
    any_space = pl.BlockSpec(memory_space=pl.ANY)
    outgoing, returning, grads = pl.pallas_call(
        functools.partial(kernel, planes, width),
        out_shape=(
            jax.ShapeDtypeStruct((row_count, width), bf16),
            jax.ShapeDtypeStruct((row_count, width), bf16),
            jax.ShapeDtypeStruct((2, shard, rank), f32),
        ),
        in_specs=[pl.BlockSpec(memory_space=pltpu.SMEM)] + [any_space] * 7,
        out_specs=(any_space, any_space, pl.BlockSpec(memory_space=pltpu.VMEM)),
        scratch_shapes=[
            pltpu.VMEM(block, bf16),
            pltpu.VMEM(block, bf16),
            pltpu.VMEM((TICKS, *block), bf16),
            pltpu.VMEM((TICKS - 1, *block), bf16),
            (pltpu.VMEM(block, bf16),) * (TICKS - 1),
            (pltpu.VMEM(block, bf16),) * (TICKS - 1),
            pltpu.VMEM((TICKS, *block), bf16),
            pltpu.VMEM((TICKS, *block), bf16),
            pltpu.VMEM((TICKS, YS, share, message), bf16),
            pltpu.VMEM((TICKS, YS - 1, share, message), bf16),
            pltpu.VMEM((TICKS, YS, share, message), bf16),
            pltpu.VMEM((columns, rank), bf16),
            pltpu.VMEM((columns, rank), bf16),
            pltpu.VMEM((2, columns, rank), f32),
            pltpu.VMEM((4, 2, shard, rank), bf16),
            pltpu.VMEM((XS, 2, shard, rank), bf16),
            dma((5 + TICKS,)),
            dma((5 + TICKS,)),
            dma((2, TICKS)),
            dma((2, TICKS)),
            dma((2, TICKS - 1)),
            dma((2, TICKS - 1)),
            dma((3,)),
            dma((3,)),
        ],
        compiler_params=pltpu.CompilerParams(
            collective_id=0, has_side_effects=True, vmem_limit_bytes=52 * 1024 * 1024
        ),
    )(
        inverse,
        carried[0, 0],
        pending[0, 0],
        stashed_inputs[0, 0],
        fresh_batches[:, 0],
        cotangent[:, 0],
        down_gained,
        up_turned,
    )
    return (
        outgoing[None, None],
        returning[None, None],
        (grads[0] * gain)[None],
        grads[1].T[None],
    )


def solution(mesh):
    planes = mesh.shape["section"] // 2
    in_specs = (
        P("section", "peer", None, None),
        P("section", "peer", None, None),
        P("section", "peer", None, None, None),
        P(None, "peer", None, None),
        P(None, "peer", None, None),
        P("section", None),
        P("section", "peer", None),
        P("section", None, "peer"),
        P(),
        P(),
    )
    out_specs = (
        P("section", "peer", None, None),
        P("section", "peer", None, None),
        P("section", "peer", None),
        P("section", None, "peer"),
    )
    return jax.shard_map(
        functools.partial(shards, planes), mesh=mesh, in_specs=in_specs, out_specs=out_specs, check_vma=False
    )
```

time: 582 us -> 200 us (0.34)
  the two profiles are of different devices: /device:TPU:4 before, /device:TPU:1 now
where the time goes in v1:
time: 200 us; the launch traced here: 197 us
  Pallas kernels  189 us (94%)
  local copies, waits for them, and re-layouts  4.79 us (2%)
  other arithmetic  3.16 us (2%)
    pallas_call x1, Pallas kernels, shards(): pl.pallas_call(functools.partial(kernel, planes, width), out_shape=(jax.S...  189 us

profile of v1, /device:TPU:1, one launch (start us, length us, event | category | flops | bytes accessed | tf_op | source)
XLA Modules:
  0.0 197.5 jit_solution(11834410236934488261)
XLA Ops:
  0.6 0.0 copy-start
  0.7 0.7 copy-done
  1.4 0.7 constant_dynamic-slice_fusion
  2.1 0.2 select_reduce_fusion.inverse
  2.3 0.8 dynamic-slice_reduce_fusion
  3.1 1.0 fusion.w_down
  4.1 0.0 copy-start.1
  4.1 0.9 copy-done.1
  5.0 188.8 %shard_map.129 = (bf16[64,5120]{1,0:T(8,128)(2,1)S(1)}, bf16[64,5120]{1,0:T(8,128)(2,1)S(1)}, f32[2,320,256]{2,1,0:T(8,128)}) custom-call(s32[6,16]{1,0:T(8,128)S(1)} %select_reduce_fusion.inverse, bf16[64,5120]{1,0:T(8,128)(2,1)} %bitcast.29, bf16[64,5120]{1,0:T(8,128)(2,1)} %bitcast.30, bf16[4,64,5120]{2,1,0:T(8,128)(2,1)} %bitcast.26, ...), custom_call_target="tpu_custom_call" | custom-call | tf_op jit(solution)/shard_map/pallas_call | solution.py:452
  193.8 1.9 slice_bitcast_fusion
  195.8 0.8 copy.20
  196.6 0.8 copy.21
  (3 shorter events, 0.0 us)
Async XLA Ops:
  0.6 0.7 copy-start
  4.1 0.9 copy-start.1

commit v2 on v1

v2 whole, which is shorter than its diff:
```python
import functools

import jax
import jax.numpy as jnp
from jax import lax
from jax.experimental import pallas as pl
from jax.experimental.pallas import tpu as pltpu
from jax.sharding import PartitionSpec as P

MESH = pl.DeviceIdType.MESH
NORM_EPS = 1e-05
TICKS = 4
XS = 4
YS = 4
PEERS = 16
LANES = 128
STEP = 256
SPARE = 16

DOWN, CARRIED, UP, PENDING, FRESH, GAIN, STASH = 0, 1, 2, 3, 4, 5, 6
F_SUM, S_SUM, B_SUM, F_ROWS, S_ROWS, B_ROWS = range(6)


def iota(shape, dim):
    return lax.broadcasted_iota(jnp.int32, shape, dim)


def to_row(column, first, length):
    shape = (column.shape[0], length)
    return jnp.sum(jnp.where(iota(shape, 1) == iota(shape, 0) + first, column, 0.0), axis=0, keepdims=True)


def to_column(row, first, count):
    shape = (count, row.shape[1])
    return jnp.sum(jnp.where(iota(shape, 1) == iota(shape, 0) + first, row, 0.0), axis=1, keepdims=True)


def in_two(row):
    high = row.astype(jnp.bfloat16).astype(jnp.float32)
    shape = (SPARE, row.shape[1])
    sub = iota(shape, 0)
    return jnp.where(sub == 0, high, jnp.where(sub == 1, row - high, 0.0)).astype(jnp.bfloat16)


def product(a, b, left, right):
    return lax.dot_general(a, b, (((left,), (right,)), ((), ())), preferred_element_type=jnp.float32)


def kernel(
    planes,
    width,
    forward_route,
    backward_route,
    carried,
    pending,
    stash,
    fresh,
    cotangent,
    gain,
    w_down,
    w_up,
    out_ref,
    ret_ref,
    down_ref,
    up_ref,
    inverse,
    gain_row,
    w_up_here,
    w_up_turned,
    x_now,
    v_now,
    u_gained,
    u_all,
    fresh_all,
    x_in,
    v_in,
    x_out,
    v_out,
    f_send,
    f_recv,
    s_send,
    s_recv,
    b_send,
    b_recv,
    f_rows,
    s_rows,
    b_rows,
    down_all,
    up_all,
    grad_sum,
    grad_send,
    grad_recv,
    local_sem,
    spread_send,
    spread_recv,
    sum_send,
    sum_recv,
    hop_send,
    hop_recv,
    last_send,
    last_recv,
):
    section = lax.axis_index("section")
    peer = lax.axis_index("peer")
    z, x_hi = section // 2, section % 2
    y, x_lo, core = peer // 4, (peer // 2) % 2, peer % 2
    x = 2 * x_hi + x_lo
    mine = 2 * z + core
    tokens, columns = x_now.shape[1], x_now.shape[2]
    shard, rank = w_down.shape
    rows = PEERS * tokens
    share = rows // YS
    home = core == x_hi
    away = core != x_hi
    is_first = mine == 0
    is_last = mine == 2 * planes - 1
    sends_last = section == 2 * planes - 1

    def place(zz, xx, yy, cc):
        return (2 * zz + xx // 2, 4 * yy + 2 * (xx % 2) + cc)

    def remote(src, dst, send_sem, recv_sem, device):
        pltpu.make_async_remote_copy(
            src_ref=src,
            dst_ref=dst,
            send_sem=send_sem,
            recv_sem=recv_sem,
            device_id=device,
            device_id_type=MESH,
        ).start()

    def settle(ref, sem):
        pltpu.make_async_copy(ref, ref, sem).wait()

    pltpu.make_async_copy(w_up, w_up_here, local_sem).start()

    barrier = pltpu.get_barrier_semaphore()
    z_up, z_down = (z + 1) % planes, (z + planes - 1) % planes

    @pl.loop(1, 32)
    def _(i):
        other = (x * 8 + y * 2 + core + i) % 32
        pl.semaphore_signal(
            barrier, inc=1, device_id=place(z, other // 8, (other // 2) % 4, other % 2), device_id_type=MESH
        )

    for zz in (z_up, z_down):
        pl.semaphore_signal(barrier, inc=1, device_id=place(zz, x, y, 1 - core), device_id_type=MESH)
    pl.semaphore_wait(barrier, 33)

    def cut_of(ref, xx, yy):
        tok = pl.ds(pl.multiple_of(xx * tokens, tokens), tokens)
        col = pl.ds(pl.multiple_of(yy * columns, LANES), columns)
        return ref.at[tok, col] if len(ref.shape) == 2 else ref.at[:, tok, col]

    def spread(source, target, k):
        sems = (spread_send.at[k], spread_recv.at[k])

        @pl.when(home)
        def _():
            pltpu.make_async_copy(cut_of(source, x, y), target.at[peer], sems[1]).start()

        @pl.when(away)
        def _():
            remote(cut_of(source, x, y), target.at[peer], *sems, place(z, x, y, x_hi))

        @pl.loop(1, XS * YS)
        def _(i):
            xx, yy = (x + i // YS) % XS, (y + i) % YS
            remote(cut_of(source, xx, yy), target.at[peer], *sems, place(z, xx, yy, x_hi))

    def spread_weight(source, target, k):
        sems = (spread_send.at[k], spread_recv.at[k])
        block = target.at[pl.ds(pl.multiple_of((2 * x_lo + core) * shard, 16), shard)]

        @pl.when(home)
        def _():
            pltpu.make_async_copy(source, block, sems[1]).start()

        @pl.when(away)
        def _():
            remote(source, block, *sems, place(z, x, y, x_hi))

        @pl.loop(1, XS)
        def _(i):
            remote(source, block, *sems, place(z, (x + i) % XS, y, x_hi))

    def settle_sent(ref, count, sem):
        @pl.when(home)
        def _():
            settle(ref.at[pl.ds(0, count - 1)], sem)

        @pl.when(away)
        def _():
            settle(ref.at[pl.ds(0, count)], sem)

    def spread_stash(t):
        @pl.when(sends_last)
        def _():
            spread(cotangent.at[t], u_all.at[t], STASH + t)

        @pl.when(jnp.logical_not(sends_last))
        def _():
            spread(stash.at[t], u_all.at[t], STASH + t)

    gain_home = jnp.logical_and(home, x == 2 * x_lo + core)
    gain_cut = gain.at[:, pl.ds(pl.multiple_of(y * columns, LANES), columns)]

    @pl.when(gain_home)
    def _():
        pltpu.make_async_copy(gain_cut, gain_row, spread_recv.at[GAIN]).start()

    @pl.when(jnp.logical_not(gain_home))
    def _():
        remote(
            gain_cut, gain_row, spread_send.at[GAIN], spread_recv.at[GAIN], place(z, 2 * x_lo + core, y, x_hi)
        )

    spread_weight(w_down, down_all, DOWN)
    spread(carried, x_now, CARRIED)
    pltpu.make_async_copy(w_up, w_up_here, local_sem).wait()
    w_up_turned[...] = w_up_here[...].T
    spread_weight(w_up_turned, up_all, UP)
    spread_stash(0)
    spread(pending, v_now, PENDING)

    @pl.when(z == 0)
    def _():
        sems = (spread_send.at[FRESH], spread_recv.at[FRESH])
        target = fresh_all.at[:, peer]

        @pl.when(core == 0)
        def _():
            pltpu.make_async_copy(cut_of(fresh, x, y), target, sems[1]).start()

        @pl.when(core == 1)
        def _():
            remote(cut_of(fresh, x, y), target, *sems, place(z, x, y, 0))

        @pl.loop(1, 2 * YS)
        def _(i):
            xx, yy = 2 * x_hi + (x_lo + i // YS) % 2, (y + i) % YS
            remote(cut_of(fresh, xx, yy), target, *sems, place(z, xx, yy, 0))

    grad_sum[...] = jnp.zeros_like(grad_sum)

    boundary = (jnp.maximum(mine - 1, 0), jnp.minimum(mine, 2 * planes - 2))
    for t in range(TICKS - 1):
        for way, route in enumerate((forward_route, backward_route)):
            goes_to = [route[t, boundary[way], q] for q in range(PEERS)]

            @pl.loop(0, PEERS)
            def _(p):
                comes_from = 0
                for q in range(1, PEERS):
                    comes_from = jnp.where(goes_to[q] == p, q, comes_from)
                inverse[way * (TICKS - 1) + t, p] = comes_from

    def flat(value):
        return value.reshape(rows, value.shape[-1])

    def times_gain(value):
        return (value.astype(jnp.float32) * gain_row[...]).astype(jnp.bfloat16)

    def squares_row(value):
        value = value.astype(jnp.float32)
        return in_two(to_row(jnp.sum(value * value, axis=-1, keepdims=True), 0, rows))

    def send_sums(source, target, kind, t):
        for i in range(1, YS):
            yy = (y + i) % YS
            remote(
                source.at[t, yy],
                target.at[t, i - 1],
                sum_send.at[kind, t],
                sum_recv.at[kind, t],
                place(z, x, yy, core),
            )

    def take_sum(source, target, kind, t):
        settle(target.at[t], sum_recv.at[kind, t])
        total = source[t, y].astype(jnp.float32)
        for i in range(YS - 1):
            total = total + target[t, i].astype(jnp.float32)
        return total

    def send_rows(target, kind, t):
        for i in range(1, YS):
            remote(
                target.at[t, y],
                target.at[t, y],
                sum_send.at[kind, t],
                sum_recv.at[kind, t],
                place(z, x, (y + i) % YS, core),
            )

    def take_rows(target, kind, t):
        settle(target.at[t, pl.ds(0, YS - 1)], sum_recv.at[kind, t])

    def scale_of(total):
        squares = to_column(total[share : share + 1] + total[share + 1 : share + 2], y * share, share)
        return lax.rsqrt(squares * (1.0 / width) + NORM_EPS)

    def put_sums(target, t, value):
        target[t, :, 0:share, :] = value.astype(jnp.bfloat16).reshape(YS, share, rank)

    def put_squares(target, t, block):
        for yy in range(YS):
            target[t, yy, share:, :] = block

    def forward_first(t):
        if t == 0:
            settle(down_all, spread_recv.at[DOWN])
            settle(gain_row, spread_recv.at[GAIN])
            settle(x_now, spread_recv.at[CARRIED])
        else:
            settle(x_in[t - 1], hop_recv.at[0, t - 1])

            @pl.when(is_first)
            def _():
                if t == 1:
                    settle(fresh_all, spread_recv.at[FRESH])
                x_now[...] = fresh_all[t - 1]

            @pl.when(jnp.logical_not(is_first))
            def _():
                for p in range(PEERS):
                    x_now[p] = x_in[t - 1][inverse[t - 1, p]]

        x_rows = flat(x_now[...])
        put_sums(f_send, t, product(times_gain(x_rows), down_all[...], 1, 0))
        put_squares(f_send, t, squares_row(x_rows))
        send_sums(f_send, f_recv, F_SUM, t)

    def forward_second(t):
        total = take_sum(f_send, f_recv, F_SUM, t)
        scale = scale_of(total)
        latent = total[0:share] * scale
        f_rows[t, y] = (latent * jax.nn.sigmoid(latent)).astype(jnp.bfloat16)
        send_rows(f_rows, F_ROWS, t)
        return latent, scale

    def forward_third(t):
        if t == 0:
            settle(up_all, spread_recv.at[UP])
        take_rows(f_rows, F_ROWS, t)
        hidden = flat(f_rows[t])
        for start in range(0, columns, STEP):
            cut = slice(start, start + STEP)
            result = flat(x_now[:, :, cut]).astype(jnp.float32) + product(hidden, up_all[cut, :], 1, 1)
            x_out[t, :, :, cut] = result.astype(jnp.bfloat16).reshape(PEERS, tokens, STEP)
            if t < TICKS - 1:
                remote(
                    x_out.at[t, :, :, cut],
                    x_in[t].at[:, :, cut],
                    hop_send.at[0, t],
                    hop_recv.at[0, t],
                    place((z + core) % planes, x, y, 1 - core),
                )
        if t == TICKS - 1:
            to_peers(x_out.at[t], out_ref, 0)

    def stash_first(t):
        settle(u_all.at[t], spread_recv.at[STASH + t])
        u_rows = flat(u_all[t])
        u_gained[...] = times_gain(u_rows)
        put_sums(s_send, t, product(u_gained[...], down_all[...], 1, 0))
        put_squares(s_send, t, squares_row(u_rows))
        send_sums(s_send, s_recv, S_SUM, t)

    def stash_second(t):
        total = take_sum(s_send, s_recv, S_SUM, t)
        scale = scale_of(total)
        latent = total[0:share] * scale
        s_rows[t, y] = (latent * jax.nn.sigmoid(latent)).astype(jnp.bfloat16)
        send_rows(s_rows, S_ROWS, t)
        return latent, scale

    def backward_first(t):
        if t == 0:
            settle(v_now, spread_recv.at[PENDING])
        else:
            settle(v_in[t - 1], hop_recv.at[1, t - 1])
            for p in range(PEERS):
                v_now[p] = v_in[t - 1][inverse[TICKS - 2 + t, p]]

        @pl.when(is_last)
        def _():
            v_now[...] = u_all[t]
            u_all[t] = x_now[...]
            u_gained[...] = times_gain(flat(x_now[...]))

        put_sums(b_send, t, product(flat(v_now[...]), up_all[...], 1, 0))
        send_sums(b_send, b_recv, B_SUM, t)

    def backward_second(t, forward_latent, stash_latent):
        total = take_sum(b_send, b_recv, B_SUM, t)
        latent = jnp.where(is_last, forward_latent[0], stash_latent[0])
        scale = jnp.where(is_last, forward_latent[1], stash_latent[1])
        sigmoid = jax.nn.sigmoid(latent)
        latent_grad = total * sigmoid * (1.0 + latent * (1.0 - sigmoid))
        b_rows[t, y, 0:share, :] = (latent_grad * scale).astype(jnp.bfloat16)
        along = jnp.sum(latent_grad * latent, axis=-1, keepdims=True) * (scale * scale * (1.0 / width))
        b_rows[t, y, share:, :] = in_two(to_row(along, y * share, rows))
        send_rows(b_rows, B_ROWS, t)

    def backward_third(t):
        take_rows(b_rows, B_ROWS, t)
        latent_grad = flat(b_rows[t, :, 0:share, :])
        extra = b_rows[t, :, share:, :].astype(jnp.float32)
        along = to_column(jnp.sum(extra[:, 0:1] + extra[:, 1:2], axis=0), 0, rows)
        for start in range(0, columns, STEP):
            cut = slice(start, start + STEP)
            result = (
                flat(v_now[:, :, cut]).astype(jnp.float32)
                + product(latent_grad, down_all[cut, :], 1, 1) * gain_row[:, cut]
                - flat(u_all[t, :, :, cut]).astype(jnp.float32) * along
            )
            v_out[t, :, :, cut] = result.astype(jnp.bfloat16).reshape(PEERS, tokens, STEP)
            if t < TICKS - 1:
                remote(
                    v_out.at[t, :, :, cut],
                    v_in[t].at[:, :, cut],
                    hop_send.at[1, t],
                    hop_recv.at[1, t],
                    place((z + core + planes - 1) % planes, x, y, 1 - core),
                )
        if t == TICKS - 1:
            to_peers(v_out.at[t], ret_ref, 1)

    def to_peers(source, target, k):
        sems = (last_send.at[k], last_recv.at[k])
        block = cut_of(target, x, y)

        @pl.when(home)
        def _():
            pltpu.make_async_copy(source.at[peer], block, sems[1]).start()

        @pl.when(away)
        def _():
            remote(source.at[peer], block, *sems, (mine, peer))

        @pl.loop(1, PEERS)
        def _(i):
            q = (peer + i) % PEERS
            remote(source.at[q], block, *sems, (mine, q))

    def grad_up(t):
        take_rows(s_rows, S_ROWS, t)
        hidden = jnp.where(is_last, flat(f_rows[t]), flat(s_rows[t]))
        for start in range(0, columns, STEP):
            cut = slice(start, start + STEP)
            grad_sum[1, cut, :] += product(flat(v_now[:, :, cut]), hidden, 0, 0)

    def grad_down(t):
        latent_grad = flat(b_rows[t, :, 0:share, :])
        for start in range(0, columns, STEP):
            cut = slice(start, start + STEP)
            grad_sum[0, cut, :] += product(u_gained[:, cut], latent_grad, 0, 0)

    def to_owners(k):
        for q in range(4):
            grad_send[k, q] = grad_sum[k, q * shard : (q + 1) * shard, :].astype(jnp.bfloat16)
        sems = (last_send.at[2 + k], last_recv.at[2 + k])
        own = 2 * x_lo + core

        @pl.when(home)
        def _():
            pltpu.make_async_copy(grad_send.at[k, own], grad_recv.at[k, x], sems[1]).start()

        @pl.when(away)
        def _():
            remote(grad_send.at[k, own], grad_recv.at[k, x], *sems, (mine, peer))

        @pl.loop(1, 4)
        def _(i):
            q = (own + i) % 4
            remote(grad_send.at[k, q], grad_recv.at[k, x], *sems, (mine, 4 * y + q))

    def owned_grad(k):
        settle(grad_recv.at[k], last_recv.at[2 + k])
        total = grad_recv[k, 0].astype(jnp.float32)
        for i in range(1, XS):
            total = total + grad_recv[k, i].astype(jnp.float32)
        return total

    for t in range(TICKS):
        forward_first(t)
        if t > 0:
            backward_third(t - 1)
        forward_latent = forward_second(t)
        if t > 0:
            grad_down(t - 1)
            stash_first(t)
        forward_third(t)
        if t == 0:
            stash_first(t)
        if t < TICKS - 1:
            spread_stash(t + 1)
        backward_first(t)
        stash_latent = stash_second(t)
        backward_second(t, forward_latent, stash_latent)
        grad_up(t)
    to_owners(1)
    backward_third(TICKS - 1)
    grad_down(TICKS - 1)
    to_owners(0)

    up_ref[...] = owned_grad(1).T
    settle(out_ref, last_recv.at[0])

    for k in (DOWN, UP):
        settle_sent(grad_send.at[0], 4, spread_send.at[k])
    for k in (CARRIED, PENDING, *range(STASH, STASH + TICKS)):
        settle_sent(x_now, PEERS, spread_send.at[k])

    @pl.when(jnp.logical_not(gain_home))
    def _():
        settle(gain_row, spread_send.at[GAIN])

    @pl.when(z == 0)
    def _():
        @pl.when(core == 0)
        def _():
            settle(fresh_all.at[:, pl.ds(0, 2 * YS - 1)], spread_send.at[FRESH])

        @pl.when(core == 1)
        def _():
            settle(fresh_all.at[:, pl.ds(0, 2 * YS)], spread_send.at[FRESH])

    for t in range(TICKS):
        for kind, ref in enumerate((f_recv, s_recv, b_recv)):
            settle(ref.at[t], sum_send.at[kind, t])
        for kind, ref in enumerate((f_rows, s_rows, b_rows)):
            settle(ref.at[t, pl.ds(0, YS - 1)], sum_send.at[F_ROWS + kind, t])
        if t < TICKS - 1:
            settle(x_out.at[t], hop_send.at[0, t])
            settle(v_out.at[t], hop_send.at[1, t])
    settle_sent(x_now, PEERS, last_send.at[0])
    settle_sent(grad_send.at[1], 4, last_send.at[3])
    down_ref[...] = owned_grad(0)
    settle(ret_ref, last_recv.at[1])
    settle_sent(x_now, PEERS, last_send.at[1])
    settle_sent(grad_send.at[0], 4, last_send.at[2])


def shards(
    planes,
    carried,
    pending,
    stashed_inputs,
    fresh_batches,
    cotangent,
    norm_gain,
    w_down,
    w_up,
    forward_route,
    backward_route,
):
    row_count, width = carried.shape[2:]
    shard, rank = w_down.shape[1:]
    tokens, columns = row_count // XS, width // YS
    rows = PEERS * tokens
    share = rows // YS

    block = (PEERS, tokens, columns)
    bf16, f32 = jnp.bfloat16, jnp.float32
    dma = pltpu.SemaphoreType.DMA
    any_space = pl.BlockSpec(memory_space=pl.ANY)
    in_vmem = pl.BlockSpec(memory_space=pltpu.VMEM)
    in_smem = pl.BlockSpec(memory_space=pltpu.SMEM)
    outgoing, returning, grad_down, grad_up = pl.pallas_call(
        functools.partial(kernel, planes, width),
        out_shape=(
            jax.ShapeDtypeStruct((row_count, width), bf16),
            jax.ShapeDtypeStruct((row_count, width), bf16),
            jax.ShapeDtypeStruct((shard, rank), f32),
            jax.ShapeDtypeStruct((rank, shard), f32),
        ),
        in_specs=[in_smem] * 2 + [any_space] * 8,
        out_specs=(any_space, any_space, in_vmem, in_vmem),
        scratch_shapes=[
            pltpu.SMEM((2 * (TICKS - 1), PEERS), jnp.int32),
            pltpu.VMEM((1, columns), f32),
            pltpu.VMEM((rank, shard), bf16),
            pltpu.VMEM((shard, rank), bf16),
            pltpu.VMEM(block, bf16),
            pltpu.VMEM(block, bf16),
            pltpu.VMEM((rows, columns), bf16),
            pltpu.VMEM((TICKS, *block), bf16),
            pltpu.VMEM((TICKS - 1, *block), bf16),
            (pltpu.VMEM(block, bf16),) * (TICKS - 1),
            (pltpu.VMEM(block, bf16),) * (TICKS - 1),
            pltpu.VMEM((TICKS, *block), bf16),
            pltpu.VMEM((TICKS, *block), bf16),
            pltpu.VMEM((TICKS, YS, share + SPARE, rank), bf16),
            pltpu.VMEM((TICKS, YS - 1, share + SPARE, rank), bf16),
            pltpu.VMEM((TICKS, YS, share + SPARE, rank), bf16),
            pltpu.VMEM((TICKS, YS - 1, share + SPARE, rank), bf16),
            pltpu.VMEM((TICKS, YS, share, rank), bf16),
            pltpu.VMEM((TICKS, YS - 1, share, rank), bf16),
            pltpu.VMEM((TICKS, YS, share, rank), bf16),
            pltpu.VMEM((TICKS, YS, share, rank), bf16),
            pltpu.VMEM((TICKS, YS, share + SPARE, rank), bf16),
            pltpu.VMEM((columns, rank), bf16),
            pltpu.VMEM((columns, rank), bf16),
            pltpu.VMEM((2, columns, rank), f32),
            pltpu.VMEM((2, 4, shard, rank), bf16),
            pltpu.VMEM((2, XS, shard, rank), bf16),
            dma(()),
            dma((STASH + TICKS,)),
            dma((STASH + TICKS,)),
            dma((6, TICKS)),
            dma((6, TICKS)),
            dma((2, TICKS - 1)),
            dma((2, TICKS - 1)),
            dma((4,)),
            dma((4,)),
        ],
        compiler_params=pltpu.CompilerParams(
            collective_id=0, has_side_effects=True, vmem_limit_bytes=52 * 1024 * 1024
        ),
    )(
        forward_route,
        backward_route,
        carried[0, 0],
        pending[0, 0],
        stashed_inputs[0, 0],
        fresh_batches[:, 0],
        cotangent[:, 0],
        norm_gain,
        w_down[0],
        w_up[0],
    )
    return outgoing[None, None], returning[None, None], grad_down[None], grad_up[None]


def solution(mesh):
    planes = mesh.shape["section"] // 2
    in_specs = (
        P("section", "peer", None, None),
        P("section", "peer", None, None),
        P("section", "peer", None, None, None),
        P(None, "peer", None, None),
        P(None, "peer", None, None),
        P("section", None),
        P("section", "peer", None),
        P("section", None, "peer"),
        P(),
        P(),
    )
    out_specs = (
        P("section", "peer", None, None),
        P("section", "peer", None, None),
        P("section", "peer", None),
        P("section", None, "peer"),
    )
    return jax.shard_map(
        functools.partial(shards, planes), mesh=mesh, in_specs=in_specs, out_specs=out_specs, check_vma=False
    )
```

time: 200 us -> 168 us (0.84)
  Pallas kernels: 189 us -> 158 us
  local copies, waits for them, and re-layouts: 4.79 us -> 8.59 us
  other arithmetic: 3.16 us -> 0 us
    pallas_call x1, Pallas kernels: 189 us -> 158 us  [shards(): pl.pallas_call(functools.partial(kernel, planes, width), out_shape=(jax.S...]
    unnamed x7 -> x13, local copies, waits for them, and re-layouts: 3.29 us -> 8.59 us
where the time goes in v2:
time: 168 us; the launch traced here: 167 us
  Pallas kernels  158 us (94%)
  local copies, waits for them, and re-layouts  8.59 us (5%)
    pallas_call x1, Pallas kernels, shards(): pl.pallas_call(functools.partial(kernel, planes, width), out_shape=(jax.S...  158 us
    unnamed x13, local copies, waits for them, and re-layouts  8.59 us

profile of v2, /device:TPU:1, one launch (start us, length us, event | category | flops | bytes accessed | tf_op | source)
XLA Modules:
  0.0 167.4 jit_solution(1914319159841632720)
XLA Ops:
  0.6 1.1 copy.14
  1.7 0.0 copy-start
  1.7 0.9 copy-done
  2.6 0.0 copy-start.1
  2.6 0.7 copy-done.1
  3.4 0.0 copy-start.2
  3.4 0.7 copy-done.2
  4.1 0.0 copy-start.3
  4.1 0.7 copy-done.3
  4.8 158.1 %shard_map.129 = (bf16[64,5120]{1,0:T(8,128)(2,1)S(1)}, bf16[64,5120]{1,0:T(8,128)(2,1)}, f32[320,256]{1,0:T(8,128)S(1)}, f32[256,320]{1,0:T(8,128)S(1)}) custom-call(s32[3,15,16]{2,1,0:T(8,128)S(1)} %copy-done.1, s32[3,15,16]{2,1,0:T(8,128)S(1)} %copy-done.2, bf16[64,5120]{1,0:T(8,128)(2,1)} %bitcast.20, bf16[64,5120]{1,0:T(8,128)(2,1)} %bitcast.21, ...), custom_call_target="tpu_custom_call" | custom-call | tf_op jit(solution)/shard_map/pallas_call | solution.py:572
  163.0 0.9 copy.15
  163.8 0.8 copy.19
  164.7 2.0 %copy.20 = bf16[1,1,64,5120]{3,2,1,0:T(8,128)(2,1)} copy(bf16[1,1,64,5120]{3,2,1,0:T(8,128)(2,1)} %bitcast.19) | data formatting | bytes 1310720
  166.6 0.7 copy.21
Async XLA Ops:
  1.7 0.9 copy-start
  2.6 0.7 copy-start.1
  3.4 0.7 copy-start.2
  4.1 0.7 copy-start.3

commit v3 on v2

--- a/solution.py
+++ b/solution.py
@@ -65,8 +65,8 @@
     up_ref,
     inverse,
     gain_row,
-    w_up_here,
-    w_up_turned,
+    forward_here,
+    backward_here,
     x_now,
     v_now,
     u_gained,
@@ -132,7 +132,12 @@
     def settle(ref, sem):
         pltpu.make_async_copy(ref, ref, sem).wait()
 
-    pltpu.make_async_copy(w_up, w_up_here, local_sem).start()
+    route_copies = [
+        pltpu.make_async_copy(route, there, local_sem.at[k])
+        for k, (route, there) in enumerate(((forward_route, forward_here), (backward_route, backward_here)))
+    ]
+    for copy in route_copies:
+        copy.start()
 
     barrier = pltpu.get_barrier_semaphore()
     z_up, z_down = (z + 1) % planes, (z + planes - 1) % planes
@@ -146,7 +151,20 @@
 
     for zz in (z_up, z_down):
         pl.semaphore_signal(barrier, inc=1, device_id=place(zz, x, y, 1 - core), device_id_type=MESH)
-    pl.semaphore_wait(barrier, 33)
+
+    @pl.when(is_first)
+    def _():
+        @pl.loop(1, planes)
+        def _(i):
+            for cc in range(2):
+                pl.semaphore_signal(
+                    barrier,
+                    inc=1,
+                    device_id=place(i, 2 * x_hi + (x_lo + i // YS) % 2, (y + 2 * YS - i) % YS, cc),
+                    device_id_type=MESH,
+                )
+
+    pl.semaphore_wait(barrier, jnp.where(z == 0, 33, 34))
 
     def cut_of(ref, xx, yy):
         tok = pl.ds(pl.multiple_of(xx * tokens, tokens), tokens)
@@ -218,35 +236,34 @@
 
     spread_weight(w_down, down_all, DOWN)
     spread(carried, x_now, CARRIED)
-    pltpu.make_async_copy(w_up, w_up_here, local_sem).wait()
-    w_up_turned[...] = w_up_here[...].T
-    spread_weight(w_up_turned, up_all, UP)
+    spread_weight(w_up, up_all, UP)
     spread_stash(0)
     spread(pending, v_now, PENDING)
 
-    @pl.when(z == 0)
-    def _():
-        sems = (spread_send.at[FRESH], spread_recv.at[FRESH])
-        target = fresh_all.at[:, peer]
-
-        @pl.when(core == 0)
-        def _():
-            pltpu.make_async_copy(cut_of(fresh, x, y), target, sems[1]).start()
-
-        @pl.when(core == 1)
-        def _():
-            remote(cut_of(fresh, x, y), target, *sems, place(z, x, y, 0))
-
-        @pl.loop(1, 2 * YS)
-        def _(i):
-            xx, yy = 2 * x_hi + (x_lo + i // YS) % 2, (y + i) % YS
-            remote(cut_of(fresh, xx, yy), target, *sems, place(z, xx, yy, 0))
+    fresh_x, fresh_y = 2 * x_hi + (x_lo + z // YS) % 2, (y + z) % YS
+    fresh_home = jnp.logical_and(z == 0, core == 0)
+
+    @pl.when(fresh_home)
+    def _():
+        pltpu.make_async_copy(cut_of(fresh, x, y), fresh_all.at[:, peer], spread_recv.at[FRESH]).start()
+
+    @pl.when(jnp.logical_not(fresh_home))
+    def _():
+        remote(
+            cut_of(fresh, fresh_x, fresh_y),
+            fresh_all.at[:, peer],
+            spread_send.at[FRESH],
+            spread_recv.at[FRESH],
+            place(0, fresh_x, fresh_y, 0),
+        )
 
     grad_sum[...] = jnp.zeros_like(grad_sum)
 
+    for copy in route_copies:
+        copy.wait()
     boundary = (jnp.maximum(mine - 1, 0), jnp.minimum(mine, 2 * planes - 2))
     for t in range(TICKS - 1):
-        for way, route in enumerate((forward_route, backward_route)):
+        for way, route in enumerate((forward_here, backward_here)):
             goes_to = [route[t, boundary[way], q] for q in range(PEERS)]
 
             @pl.loop(0, PEERS)
@@ -445,9 +462,11 @@
             q = (peer + i) % PEERS
             remote(source.at[q], block, *sems, (mine, q))
 
-    def grad_up(t):
+    def grad_up(t, may_be_last):
         take_rows(s_rows, S_ROWS, t)
-        hidden = jnp.where(is_last, flat(f_rows[t]), flat(s_rows[t]))
+        hidden = flat(s_rows[t])
+        if may_be_last:
+            hidden = jnp.where(is_last, flat(f_rows[t]), hidden)
         for start in range(0, columns, STEP):
             cut = slice(start, start + STEP)
             grad_sum[1, cut, :] += product(flat(v_now[:, :, cut]), hidden, 0, 0)
@@ -484,29 +503,58 @@
             total = total + grad_recv[k, i].astype(jnp.float32)
         return total
 
-    for t in range(TICKS):
-        forward_first(t)
-        if t > 0:
-            backward_third(t - 1)
-        forward_latent = forward_second(t)
-        if t > 0:
-            grad_down(t - 1)
+    forward_first(0)
+    latent = forward_second(0)
+    forward_third(0)
+    spread_stash(1)
+    stash_first(0)
+    backward_first(0)
+    backward_second(0, latent, stash_second(0))
+    grad_up(0, True)
+    backward_third(0)
+    grad_down(0)
+
+    @pl.when(core == 0)
+    def _():
+        for t in range(1, TICKS):
             stash_first(t)
-        forward_third(t)
-        if t == 0:
+            if t < TICKS - 1:
+                spread_stash(t + 1)
+            backward_first(t)
+            latent = stash_second(t)
+            backward_second(t, latent, latent)
+            forward_first(t)
+            grad_up(t, False)
+            if t == TICKS - 1:
+                to_owners(1)
+            backward_third(t)
+            forward_second(t)
+            grad_down(t)
+            if t == TICKS - 1:
+                to_owners(0)
+            forward_third(t)
+
+    @pl.when(core == 1)
+    def _():
+        for t in range(1, TICKS):
             stash_first(t)
-        if t < TICKS - 1:
-            spread_stash(t + 1)
-        backward_first(t)
-        stash_latent = stash_second(t)
-        backward_second(t, forward_latent, stash_latent)
-        grad_up(t)
-    to_owners(1)
-    backward_third(TICKS - 1)
-    grad_down(TICKS - 1)
-    to_owners(0)
-
-    up_ref[...] = owned_grad(1).T
+            if t < TICKS - 1:
+                spread_stash(t + 1)
+            forward_first(t)
+            backward_first(t)
+            stash_latent = stash_second(t)
+            latent = forward_second(t)
+            backward_second(t, latent, stash_latent)
+            forward_third(t)
+            grad_up(t, True)
+            if t == TICKS - 1:
+                to_owners(1)
+            backward_third(t)
+            grad_down(t)
+            if t == TICKS - 1:
+                to_owners(0)
+
+    up_ref[...] = owned_grad(1)
     settle(out_ref, last_recv.at[0])
 
     for k in (DOWN, UP):
@@ -518,15 +566,9 @@
     def _():
         settle(gain_row, spread_send.at[GAIN])
 
-    @pl.when(z == 0)
-    def _():
-        @pl.when(core == 0)
-        def _():
-            settle(fresh_all.at[:, pl.ds(0, 2 * YS - 1)], spread_send.at[FRESH])
-
-        @pl.when(core == 1)
-        def _():
-            settle(fresh_all.at[:, pl.ds(0, 2 * YS)], spread_send.at[FRESH])
+    @pl.when(jnp.logical_not(fresh_home))
+    def _():
+        settle(fresh_all.at[:, 0], spread_send.at[FRESH])
 
     for t in range(TICKS):
         for kind, ref in enumerate((f_recv, s_recv, b_recv)):
@@ -562,28 +604,28 @@
     tokens, columns = row_count // XS, width // YS
     rows = PEERS * tokens
     share = rows // YS
+    assert planes == 2 * YS
 
     block = (PEERS, tokens, columns)
     bf16, f32 = jnp.bfloat16, jnp.float32
     dma = pltpu.SemaphoreType.DMA
-    any_space = pl.BlockSpec(memory_space=pl.ANY)
+    in_hbm = pl.BlockSpec(memory_space=pltpu.HBM)
     in_vmem = pl.BlockSpec(memory_space=pltpu.VMEM)
-    in_smem = pl.BlockSpec(memory_space=pltpu.SMEM)
     outgoing, returning, grad_down, grad_up = pl.pallas_call(
         functools.partial(kernel, planes, width),
         out_shape=(
             jax.ShapeDtypeStruct((row_count, width), bf16),
             jax.ShapeDtypeStruct((row_count, width), bf16),
             jax.ShapeDtypeStruct((shard, rank), f32),
-            jax.ShapeDtypeStruct((rank, shard), f32),
+            jax.ShapeDtypeStruct((shard, rank), f32),
         ),
-        in_specs=[in_smem] * 2 + [any_space] * 8,
-        out_specs=(any_space, any_space, in_vmem, in_vmem),
+        in_specs=[in_hbm] * 10,
+        out_specs=(in_hbm, in_hbm, in_vmem, in_vmem),
         scratch_shapes=[
             pltpu.SMEM((2 * (TICKS - 1), PEERS), jnp.int32),
             pltpu.VMEM((1, columns), f32),
-            pltpu.VMEM((rank, shard), bf16),
-            pltpu.VMEM((shard, rank), bf16),
+            pltpu.SMEM(forward_route.shape, jnp.int32),
+            pltpu.SMEM(backward_route.shape, jnp.int32),
             pltpu.VMEM(block, bf16),
             pltpu.VMEM(block, bf16),
             pltpu.VMEM((rows, columns), bf16),
@@ -607,7 +649,7 @@
             pltpu.VMEM((2, columns, rank), f32),
             pltpu.VMEM((2, 4, shard, rank), bf16),
             pltpu.VMEM((2, XS, shard, rank), bf16),
-            dma(()),
+            dma((2,)),
             dma((STASH + TICKS,)),
             dma((STASH + TICKS,)),
             dma((6, TICKS)),
@@ -618,7 +660,7 @@
             dma((4,)),
         ],
         compiler_params=pltpu.CompilerParams(
-            collective_id=0, has_side_effects=True, vmem_limit_bytes=52 * 1024 * 1024
+            collective_id=0, has_side_effects=True, vmem_limit_bytes=56 * 1024 * 1024
         ),
     )(
         forward_route,
@@ -630,9 +672,9 @@
         cotangent[:, 0],
         norm_gain,
         w_down[0],
-        w_up[0],
+        w_up[0].T,
     )
-    return outgoing[None, None], returning[None, None], grad_down[None], grad_up[None]
+    return outgoing[None, None], returning[None, None], grad_down[None], grad_up.T[None]
 
 
 def solution(mesh):

time: 168 us -> 171 us (1.018)
  Pallas kernels: 158 us -> 165 us
  local copies, waits for them, and re-layouts: 8.59 us -> 5.45 us
    pallas_call x1, Pallas kernels: 158 us -> 165 us  [shards(): pl.pallas_call(functools.partial(kernel, planes, width), out_shape=(jax.S...]
    unnamed x13 -> x8, local copies, waits for them, and re-layouts: 8.59 us -> 5.45 us
where the time goes in v3:
time: 171 us
  Pallas kernels  165 us (96%)
  local copies, waits for them, and re-layouts  5.45 us (3%)
    pallas_call x1, Pallas kernels, shards(): pl.pallas_call(functools.partial(kernel, planes, width), out_shape=(jax.S...  165 us
    unnamed x8, local copies, waits for them, and re-layouts  5.45 us

profile of v3, /device:TPU:1, one launch (start us, length us, event | category | flops | bytes accessed | tf_op | source)
XLA Modules:
  0.0 170.8 jit_solution(8300473840239017345)
XLA Ops:
  0.6 164.7 %shard_map.129 = (bf16[64,5120]{1,0:T(8,128)(2,1)}, bf16[64,5120]{1,0:T(8,128)(2,1)}, f32[320,256]{1,0:T(8,128)}, f32[320,256]{1,0:T(8,128)}) custom-call(s32[3,15,16]{2,1,0:T(8,128)} %forward_route.1, s32[3,15,16]{2,1,0:T(8,128)} %backward_route.1, bf16[64,5120]{1,0:T(8,128)(2,1)} %bitcast.20, bf16[64,5120]{1,0:T(8,128)(2,1)} %bitcast.21, ...), custom_call_target="tpu_custom_call" | custom-call | tf_op jit(solution)/shard_map/pallas_call | solution.py:614
  165.3 0.0 copy-start.1
  165.4 0.0 copy-start
  165.4 2.0 %copy.18 = bf16[1,1,64,5120]{3,2,1,0:T(8,128)(2,1)} copy(bf16[1,1,64,5120]{3,2,1,0:T(8,128)(2,1)} %bitcast.19) | data formatting | bytes 1310720
  167.4 2.0 %copy.19 = bf16[1,1,64,5120]{3,2,1,0:T(8,128)(2,1)} copy(bf16[1,1,64,5120]{3,2,1,0:T(8,128)(2,1)} %bitcast.18) | data formatting | bytes 1310720
  169.4 0.0 copy-done.1
  169.4 0.7 copy.20
  170.1 0.0 copy-done
  170.1 0.7 copy.21
Async XLA Ops:
  165.3 4.0 %copy-start.1 = (f32[320,256]{1,0:T(8,128)S(1)}, f32[320,256]{1,0:T(8,128)}, u32[]{:S(2)}) copy-start(f32[320,256]{1,0:T(8,128)} %get-tuple-element.10) | copy-start | bytes 983044
  165.4 4.7 %copy-start = (f32[320,256]{1,0:T(8,128)S(1)}, f32[320,256]{1,0:T(8,128)}, u32[]{:S(2)}) copy-start(f32[320,256]{1,0:T(8,128)} %get-tuple-element.11) | copy-start | bytes 983044

commit v4 on v2

--- a/solution.py
+++ b/solution.py
@@ -17,7 +17,7 @@
 STEP = 256
 SPARE = 16
 
-DOWN, CARRIED, UP, PENDING, FRESH, GAIN, STASH = 0, 1, 2, 3, 4, 5, 6
+DOWN, CARRIED, UP, PENDING, GAIN, FRESH, RELAY, STASH = 0, 1, 2, 3, 4, 5, 8, 11
 F_SUM, S_SUM, B_SUM, F_ROWS, S_ROWS, B_ROWS = range(6)
 
 
@@ -65,13 +65,14 @@
     up_ref,
     inverse,
     gain_row,
-    w_up_here,
-    w_up_turned,
+    forward_here,
+    backward_here,
     x_now,
     v_now,
     u_gained,
     u_all,
     fresh_all,
+    relay,
     x_in,
     v_in,
     x_out,
@@ -132,7 +133,12 @@
     def settle(ref, sem):
         pltpu.make_async_copy(ref, ref, sem).wait()
 
-    pltpu.make_async_copy(w_up, w_up_here, local_sem).start()
+    route_copies = [
+        pltpu.make_async_copy(route, there, local_sem.at[k])
+        for k, (route, there) in enumerate(((forward_route, forward_here), (backward_route, backward_here)))
+    ]
+    for copy in route_copies:
+        copy.start()
 
     barrier = pltpu.get_barrier_semaphore()
     z_up, z_down = (z + 1) % planes, (z + planes - 1) % planes
@@ -146,25 +152,36 @@
 
     for zz in (z_up, z_down):
         pl.semaphore_signal(barrier, inc=1, device_id=place(zz, x, y, 1 - core), device_id_type=MESH)
-    pl.semaphore_wait(barrier, 33)
+
+
+    @pl.when(is_first)
+    def _():
+        @pl.loop(1, planes)
+        def _(i):
+            for cc in range(2):
+                pl.semaphore_signal(barrier, inc=1, device_id=place(i, x, y, cc), device_id_type=MESH)
+
+    pl.semaphore_wait(barrier, jnp.where(z == 0, 33, 34))
 
     def cut_of(ref, xx, yy):
         tok = pl.ds(pl.multiple_of(xx * tokens, tokens), tokens)
         col = pl.ds(pl.multiple_of(yy * columns, LANES), columns)
         return ref.at[tok, col] if len(ref.shape) == 2 else ref.at[:, tok, col]
 
-    def spread(source, target, k):
+    def spread(source, target, k, first=0, count=XS * YS):
         sems = (spread_send.at[k], spread_recv.at[k])
 
-        @pl.when(home)
-        def _():
-            pltpu.make_async_copy(cut_of(source, x, y), target.at[peer], sems[1]).start()
-
-        @pl.when(away)
-        def _():
-            remote(cut_of(source, x, y), target.at[peer], *sems, place(z, x, y, x_hi))
-
-        @pl.loop(1, XS * YS)
+        if first == 0:
+
+            @pl.when(home)
+            def _():
+                pltpu.make_async_copy(cut_of(source, x, y), target.at[peer], sems[1]).start()
+
+            @pl.when(away)
+            def _():
+                remote(cut_of(source, x, y), target.at[peer], *sems, place(z, x, y, x_hi))
+
+        @pl.loop(max(first, 1), first + count)
         def _(i):
             xx, yy = (x + i // YS) % XS, (y + i) % YS
             remote(cut_of(source, xx, yy), target.at[peer], *sems, place(z, xx, yy, x_hi))
@@ -194,14 +211,54 @@
         def _():
             settle(ref.at[pl.ds(0, count)], sem)
 
-    def spread_stash(t):
+    def fresh_shift(t):
+        shift = (z + (TICKS - 1) * t) % planes
+        return shift // YS, shift % YS
+
+    def relay_fresh(t):
+        by_x, by_y = fresh_shift(t)
+        xx, yy = 2 * x_hi + (x_lo + by_x) % 2, (y + by_y) % YS
+        stays = by_x + by_y == 0
+
+        @pl.when(stays)
+        def _():
+            pltpu.make_async_copy(cut_of(fresh.at[t], x, y), relay.at[t], spread_recv.at[RELAY + t]).start()
+
+        @pl.when(jnp.logical_not(stays))
+        def _():
+            remote(
+                cut_of(fresh.at[t], xx, yy),
+                relay.at[t],
+                spread_send.at[RELAY + t],
+                spread_recv.at[RELAY + t],
+                place(z, xx, yy, core),
+            )
+
+    def drop_fresh(t):
+        by_x, by_y = fresh_shift(t)
+        settle(relay.at[t], spread_recv.at[RELAY + t])
+        target = fresh_all.at[t, 4 * ((y + YS - by_y) % YS) + 2 * ((x_lo + 2 - by_x) % 2) + core]
+
+        @pl.when(is_first)
+        def _():
+            pltpu.make_async_copy(relay.at[t], target, spread_recv.at[FRESH + t]).start()
+
+        @pl.when(jnp.logical_not(is_first))
+        def _():
+            remote(relay.at[t], target, spread_send.at[FRESH + t], spread_recv.at[FRESH + t], place(0, x, y, 0))
+
+    def spread_stash(t, *parts):
         @pl.when(sends_last)
         def _():
-            spread(cotangent.at[t], u_all.at[t], STASH + t)
+            spread(cotangent.at[t], u_all.at[t], STASH + t, *parts)
 
         @pl.when(jnp.logical_not(sends_last))
         def _():
-            spread(stash.at[t], u_all.at[t], STASH + t)
+            spread(stash.at[t], u_all.at[t], STASH + t, *parts)
+
+    def stash_part(t, part):
+        if 0 < t < TICKS - 1:
+            spread_stash(t + 1, 4 * part, 4)
 
     gain_home = jnp.logical_and(home, x == 2 * x_lo + core)
     gain_cut = gain.at[:, pl.ds(pl.multiple_of(y * columns, LANES), columns)]
@@ -216,37 +273,23 @@
             gain_cut, gain_row, spread_send.at[GAIN], spread_recv.at[GAIN], place(z, 2 * x_lo + core, y, x_hi)
         )
 
+    for t in range(TICKS - 1):
+        relay_fresh(t)
     spread_weight(w_down, down_all, DOWN)
     spread(carried, x_now, CARRIED)
-    pltpu.make_async_copy(w_up, w_up_here, local_sem).wait()
-    w_up_turned[...] = w_up_here[...].T
-    spread_weight(w_up_turned, up_all, UP)
+    spread_weight(w_up, up_all, UP)
     spread_stash(0)
     spread(pending, v_now, PENDING)
-
-    @pl.when(z == 0)
-    def _():
-        sems = (spread_send.at[FRESH], spread_recv.at[FRESH])
-        target = fresh_all.at[:, peer]
-
-        @pl.when(core == 0)
-        def _():
-            pltpu.make_async_copy(cut_of(fresh, x, y), target, sems[1]).start()
-
-        @pl.when(core == 1)
-        def _():
-            remote(cut_of(fresh, x, y), target, *sems, place(z, x, y, 0))
-
-        @pl.loop(1, 2 * YS)
-        def _(i):
-            xx, yy = 2 * x_hi + (x_lo + i // YS) % 2, (y + i) % YS
-            remote(cut_of(fresh, xx, yy), target, *sems, place(z, xx, yy, 0))
+    for t in range(TICKS - 1):
+        drop_fresh(t)
 
     grad_sum[...] = jnp.zeros_like(grad_sum)
 
+    for copy in route_copies:
+        copy.wait()
     boundary = (jnp.maximum(mine - 1, 0), jnp.minimum(mine, 2 * planes - 2))
     for t in range(TICKS - 1):
-        for way, route in enumerate((forward_route, backward_route)):
+        for way, route in enumerate((forward_here, backward_here)):
             goes_to = [route[t, boundary[way], q] for q in range(PEERS)]
 
             @pl.loop(0, PEERS)
@@ -318,8 +361,7 @@
 
             @pl.when(is_first)
             def _():
-                if t == 1:
-                    settle(fresh_all, spread_recv.at[FRESH])
+                settle(fresh_all.at[t - 1], spread_recv.at[FRESH + t - 1])
                 x_now[...] = fresh_all[t - 1]
 
             @pl.when(jnp.logical_not(is_first))
@@ -327,6 +369,7 @@
                 for p in range(PEERS):
                     x_now[p] = x_in[t - 1][inverse[t - 1, p]]
 
+        stash_part(t, 0)
         x_rows = flat(x_now[...])
         put_sums(f_send, t, product(times_gain(x_rows), down_all[...], 1, 0))
         put_squares(f_send, t, squares_row(x_rows))
@@ -344,6 +387,7 @@
         if t == 0:
             settle(up_all, spread_recv.at[UP])
         take_rows(f_rows, F_ROWS, t)
+        stash_part(t, 2)
         hidden = flat(f_rows[t])
         for start in range(0, columns, STEP):
             cut = slice(start, start + STEP)
@@ -384,6 +428,8 @@
             for p in range(PEERS):
                 v_now[p] = v_in[t - 1][inverse[TICKS - 2 + t, p]]
 
+        stash_part(t, 3)
+
         @pl.when(is_last)
         def _():
             v_now[...] = u_all[t]
@@ -406,6 +452,7 @@
 
     def backward_third(t):
         take_rows(b_rows, B_ROWS, t)
+        stash_part(t + 1, 1)
         latent_grad = flat(b_rows[t, :, 0:share, :])
         extra = b_rows[t, :, share:, :].astype(jnp.float32)
         along = to_column(jnp.sum(extra[:, 0:1] + extra[:, 1:2], axis=0), 0, rows)
@@ -488,25 +535,30 @@
         forward_first(t)
         if t > 0:
             backward_third(t - 1)
-        forward_latent = forward_second(t)
+        latent = forward_second(t)
         if t > 0:
             grad_down(t - 1)
             stash_first(t)
         forward_third(t)
         if t == 0:
-            stash_first(t)
+            spread_stash(1)
+            stash_first(0)
         if t < TICKS - 1:
-            spread_stash(t + 1)
-        backward_first(t)
-        stash_latent = stash_second(t)
-        backward_second(t, forward_latent, stash_latent)
-        grad_up(t)
-    to_owners(1)
+            backward_first(t)
+            stash_latent = stash_second(t)
+            backward_second(t, latent, stash_latent)
+            grad_up(t)
+        else:
+            stash_latent = stash_second(t)
+            backward_first(t)
+            grad_up(t)
+            to_owners(1)
+            backward_second(t, latent, stash_latent)
     backward_third(TICKS - 1)
     grad_down(TICKS - 1)
     to_owners(0)
 
-    up_ref[...] = owned_grad(1).T
+    up_ref[...] = owned_grad(1)
     settle(out_ref, last_recv.at[0])
 
     for k in (DOWN, UP):
@@ -518,15 +570,16 @@
     def _():
         settle(gain_row, spread_send.at[GAIN])
 
-    @pl.when(z == 0)
-    def _():
-        @pl.when(core == 0)
-        def _():
-            settle(fresh_all.at[:, pl.ds(0, 2 * YS - 1)], spread_send.at[FRESH])
-
-        @pl.when(core == 1)
-        def _():
-            settle(fresh_all.at[:, pl.ds(0, 2 * YS)], spread_send.at[FRESH])
+    for t in range(TICKS - 1):
+        by_x, by_y = fresh_shift(t)
+
+        @pl.when(by_x + by_y > 0)
+        def _():
+            settle(relay.at[t], spread_send.at[RELAY + t])
+
+        @pl.when(jnp.logical_not(is_first))
+        def _():
+            settle(relay.at[t], spread_send.at[FRESH + t])
 
     for t in range(TICKS):
         for kind, ref in enumerate((f_recv, s_recv, b_recv)):
@@ -566,29 +619,29 @@
     block = (PEERS, tokens, columns)
     bf16, f32 = jnp.bfloat16, jnp.float32
     dma = pltpu.SemaphoreType.DMA
-    any_space = pl.BlockSpec(memory_space=pl.ANY)
+    in_hbm = pl.BlockSpec(memory_space=pltpu.HBM)
     in_vmem = pl.BlockSpec(memory_space=pltpu.VMEM)
-    in_smem = pl.BlockSpec(memory_space=pltpu.SMEM)
     outgoing, returning, grad_down, grad_up = pl.pallas_call(
         functools.partial(kernel, planes, width),
         out_shape=(
-            jax.ShapeDtypeStruct((row_count, width), bf16),
-            jax.ShapeDtypeStruct((row_count, width), bf16),
-            jax.ShapeDtypeStruct((shard, rank), f32),
-            jax.ShapeDtypeStruct((rank, shard), f32),
+            pltpu.VMEM((row_count, width), bf16),
+            pltpu.VMEM((row_count, width), bf16),
+            pltpu.VMEM((shard, rank), f32),
+            pltpu.VMEM((shard, rank), f32),
         ),
-        in_specs=[in_smem] * 2 + [any_space] * 8,
-        out_specs=(any_space, any_space, in_vmem, in_vmem),
+        in_specs=[in_hbm] * 10,
+        out_specs=(in_vmem,) * 4,
         scratch_shapes=[
             pltpu.SMEM((2 * (TICKS - 1), PEERS), jnp.int32),
             pltpu.VMEM((1, columns), f32),
-            pltpu.VMEM((rank, shard), bf16),
-            pltpu.VMEM((shard, rank), bf16),
+            pltpu.SMEM(forward_route.shape, jnp.int32),
+            pltpu.SMEM(backward_route.shape, jnp.int32),
             pltpu.VMEM(block, bf16),
             pltpu.VMEM(block, bf16),
             pltpu.VMEM((rows, columns), bf16),
             pltpu.VMEM((TICKS, *block), bf16),
             pltpu.VMEM((TICKS - 1, *block), bf16),
+            pltpu.VMEM((TICKS - 1, *block[1:]), bf16),
             (pltpu.VMEM(block, bf16),) * (TICKS - 1),
             (pltpu.VMEM(block, bf16),) * (TICKS - 1),
             pltpu.VMEM((TICKS, *block), bf16),
@@ -607,7 +660,7 @@
             pltpu.VMEM((2, columns, rank), f32),
             pltpu.VMEM((2, 4, shard, rank), bf16),
             pltpu.VMEM((2, XS, shard, rank), bf16),
-            dma(()),
+            dma((2,)),
             dma((STASH + TICKS,)),
             dma((STASH + TICKS,)),
             dma((6, TICKS)),
@@ -618,9 +671,9 @@
             dma((4,)),
         ],
         compiler_params=pltpu.CompilerParams(
-            collective_id=0, has_side_effects=True, vmem_limit_bytes=52 * 1024 * 1024
+            collective_id=0, has_side_effects=True, vmem_limit_bytes=50 * 1024 * 1024
         ),
-    )(
+    )(*(pltpu.with_memory_space_constraint(a, pltpu.HBM) for a in (
         forward_route,
         backward_route,
         carried[0, 0],
@@ -630,9 +683,9 @@
         cotangent[:, 0],
         norm_gain,
         w_down[0],
-        w_up[0],
-    )
-    return outgoing[None, None], returning[None, None], grad_down[None], grad_up[None]
+        w_up[0].T,
+    )))
+    return outgoing[None, None], returning[None, None], grad_down[None], grad_up.T[None]
 
 
 def solution(mesh):

time: 168 us -> 157 us (0.935); the launches traced: 167 us -> 154 us
  Pallas kernels: 158 us -> 151 us
  local copies, waits for them, and re-layouts: 8.59 us -> 3.12 us
    pallas_call x1, Pallas kernels: 158 us -> 151 us  [shards(): pl.pallas_call(functools.partial(kernel, planes, width), out_shape=(pltpu...]
    unnamed x13 -> x4, local copies, waits for them, and re-layouts: 8.59 us -> 3.12 us
where the time goes in v4:
time: 157 us; the launch traced here: 154 us
  Pallas kernels  151 us (96%)
  local copies, waits for them, and re-layouts  3.12 us (2%)
    pallas_call x1, Pallas kernels, shards(): pl.pallas_call(functools.partial(kernel, planes, width), out_shape=(pltpu...  151 us

profile of v4, /device:TPU:1, one launch (start us, length us, event | category | flops | bytes accessed | tf_op | source)
XLA Modules:
  0.0 154.4 jit_solution(7001107043121820523)
XLA Ops:
  0.6 150.6 %shard_map.129 = (bf16[64,5120]{1,0:T(8,128)(2,1)S(1)}, bf16[64,5120]{1,0:T(8,128)(2,1)S(1)}, f32[320,256]{1,0:T(8,128)S(1)}, f32[320,256]{1,0:T(8,128)S(1)}) custom-call(s32[3,15,16]{2,1,0:T(8,128)} %forward_route.1, s32[3,15,16]{2,1,0:T(8,128)} %backward_route.1, bf16[64,5120]{1,0:T(8,128)(2,1)} %bitcast.22, bf16[64,5120]{1,0:T(8,128)(2,1)} %bitcast.23, ...), custom_call_target="tpu_custom_call" | custom-call | tf_op jit(solution)/shard_map/pallas_call | solution.py:624
  151.2 0.8 copy.18
  152.1 0.8 copy.19
  152.9 0.7 copy.20
  153.6 0.7 copy.21

commit v5 on v4

--- a/solution.py
+++ b/solution.py
@@ -258,7 +258,8 @@
 
     def stash_part(t, part):
         if 0 < t < TICKS - 1:
-            spread_stash(t + 1, 4 * part, 4)
+            if part == 0:
+                spread_stash(t + 1)
 
     gain_home = jnp.logical_and(home, x == 2 * x_lo + core)
     gain_cut = gain.at[:, pl.ds(pl.multiple_of(y * columns, LANES), columns)]
@@ -369,7 +370,7 @@
                 for p in range(PEERS):
                     x_now[p] = x_in[t - 1][inverse[t - 1, p]]
 
-        stash_part(t, 0)
+        stash_part(t - 1, 3)
         x_rows = flat(x_now[...])
         put_sums(f_send, t, product(times_gain(x_rows), down_all[...], 1, 0))
         put_squares(f_send, t, squares_row(x_rows))
@@ -387,7 +388,7 @@
         if t == 0:
             settle(up_all, spread_recv.at[UP])
         take_rows(f_rows, F_ROWS, t)
-        stash_part(t, 2)
+        stash_part(t, 1)
         hidden = flat(f_rows[t])
         for start in range(0, columns, STEP):
             cut = slice(start, start + STEP)
@@ -428,7 +429,7 @@
             for p in range(PEERS):
                 v_now[p] = v_in[t - 1][inverse[TICKS - 2 + t, p]]
 
-        stash_part(t, 3)
+        stash_part(t, 2)
 
         @pl.when(is_last)
         def _():
@@ -452,7 +453,7 @@
 
     def backward_third(t):
         take_rows(b_rows, B_ROWS, t)
-        stash_part(t + 1, 1)
+        stash_part(t + 1, 0)
         latent_grad = flat(b_rows[t, :, 0:share, :])
         extra = b_rows[t, :, share:, :].astype(jnp.float32)
         along = to_column(jnp.sum(extra[:, 0:1] + extra[:, 1:2], axis=0), 0, rows)
@@ -531,31 +532,30 @@
             total = total + grad_recv[k, i].astype(jnp.float32)
         return total
 
-    for t in range(TICKS):
-        forward_first(t)
-        if t > 0:
-            backward_third(t - 1)
-        latent = forward_second(t)
-        if t > 0:
-            grad_down(t - 1)
-            stash_first(t)
-        forward_third(t)
-        if t == 0:
-            spread_stash(1)
-            stash_first(0)
-        if t < TICKS - 1:
-            backward_first(t)
-            stash_latent = stash_second(t)
-            backward_second(t, latent, stash_latent)
-            grad_up(t)
-        else:
-            stash_latent = stash_second(t)
-            backward_first(t)
-            grad_up(t)
-            to_owners(1)
-            backward_second(t, latent, stash_latent)
-    backward_third(TICKS - 1)
-    grad_down(TICKS - 1)
+    forward_first(0)
+    latent = forward_second(0)
+    forward_third(0)
+    spread_stash(1)
+    stash_first(0)
+    for t in range(TICKS - 1):
+        backward_first(t)
+        forward_first(t + 1)
+        stash_latent = stash_second(t)
+        backward_second(t, latent, stash_latent)
+        latent = forward_second(t + 1)
+        grad_up(t)
+        backward_third(t)
+        forward_third(t + 1)
+        grad_down(t)
+        stash_first(t + 1)
+    last = TICKS - 1
+    stash_latent = stash_second(last)
+    backward_first(last)
+    grad_up(last)
+    to_owners(1)
+    backward_second(last, latent, stash_latent)
+    backward_third(last)
+    grad_down(last)
     to_owners(0)
 
     up_ref[...] = owned_grad(1)

time: 157 us -> 148 us (0.943); the launches traced: 154 us -> 148 us
  Pallas kernels: 151 us -> 145 us
    pallas_call x1, Pallas kernels: 151 us -> 145 us  [shards(): pl.pallas_call(functools.partial(kernel, planes, width), out_shape=(pltpu...]
where the time goes in v5:
time: 148 us
  Pallas kernels  145 us (98%)
  local copies, waits for them, and re-layouts  3.12 us (2%)
    pallas_call x1, Pallas kernels, shards(): pl.pallas_call(functools.partial(kernel, planes, width), out_shape=(pltpu...  145 us
    unnamed x4, local copies, waits for them, and re-layouts  3.12 us

profile of v5, /device:TPU:1, one launch (start us, length us, event | category | flops | bytes accessed | tf_op | source)
XLA Modules:
  0.0 148.3 jit_solution(11063714882739311471)
XLA Ops:
  0.6 144.5 %shard_map.129 = (bf16[64,5120]{1,0:T(8,128)(2,1)S(1)}, bf16[64,5120]{1,0:T(8,128)(2,1)S(1)}, f32[320,256]{1,0:T(8,128)S(1)}, f32[320,256]{1,0:T(8,128)S(1)}) custom-call(s32[3,15,16]{2,1,0:T(8,128)} %forward_route.1, s32[3,15,16]{2,1,0:T(8,128)} %backward_route.1, bf16[64,5120]{1,0:T(8,128)(2,1)} %bitcast.22, bf16[64,5120]{1,0:T(8,128)(2,1)} %bitcast.23, ...), custom_call_target="tpu_custom_call" | custom-call | tf_op jit(solution)/shard_map/pallas_call | solution.py:624
  145.2 0.8 copy.18
  146.0 0.8 copy.19
  146.8 0.7 copy.20
  147.6 0.7 copy.21

commit v6 on v5

--- a/solution.py
+++ b/solution.py
@@ -183,7 +183,7 @@
 
         @pl.loop(max(first, 1), first + count)
         def _(i):
-            xx, yy = (x + i // YS) % XS, (y + i) % YS
+            xx, yy = (x + i) % XS, (y + i // XS + i) % YS
             remote(cut_of(source, xx, yy), target.at[peer], *sems, place(z, xx, yy, x_hi))
 
     def spread_weight(source, target, k):

time: 148 us -> 148 us (level); the launches traced: 148 us -> 147 us
  Pallas kernels: 145 us -> 143 us
    pallas_call x1, Pallas kernels: 145 us -> 143 us  [shards(): pl.pallas_call(functools.partial(kernel, planes, width), out_shape=(pltpu...]
where the time goes in v6:
time: 148 us; the launch traced here: 147 us
  Pallas kernels  143 us (97%)
  local copies, waits for them, and re-layouts  3.12 us (2%)
    pallas_call x1, Pallas kernels, shards(): pl.pallas_call(functools.partial(kernel, planes, width), out_shape=(pltpu...  143 us
    unnamed x4, local copies, waits for them, and re-layouts  3.12 us

profile of v6, /device:TPU:1, one launch (start us, length us, event | category | flops | bytes accessed | tf_op | source)
XLA Modules:
  0.0 146.8 jit_solution(11007254169398177199)
XLA Ops:
  0.6 143.0 %shard_map.129 = (bf16[64,5120]{1,0:T(8,128)(2,1)S(1)}, bf16[64,5120]{1,0:T(8,128)(2,1)S(1)}, f32[320,256]{1,0:T(8,128)S(1)}, f32[320,256]{1,0:T(8,128)S(1)}) custom-call(s32[3,15,16]{2,1,0:T(8,128)} %forward_route.1, s32[3,15,16]{2,1,0:T(8,128)} %backward_route.1, bf16[64,5120]{1,0:T(8,128)(2,1)} %bitcast.22, bf16[64,5120]{1,0:T(8,128)(2,1)} %bitcast.23, ...), custom_call_target="tpu_custom_call" | custom-call | tf_op jit(solution)/shard_map/pallas_call | solution.py:624
  143.6 0.8 copy.18
  144.5 0.8 copy.19
  145.3 0.7 copy.20
  146.0 0.7 copy.21
